TPU v7x, 32 devices: a whole 2x2x4 slice. The times are simulated.
32 devices in a mesh: fsdp: 4 (over y, x), tensor: 8 (over z, core).
Axes of the slice: x: 2, y: 2, z: 4, core: 2. Of those that a mesh axis runs over, the one named last changes fastest.
Arguments:
- tokens: bfloat16 [768, 8192], P(('fsdp', 'tensor')), may hold values from -6 to 6
- out_grad: bfloat16 [768, 8192], P(('fsdp', 'tensor')), may hold values from -6 to 6
- up_weight: bfloat16 [256, 8, 128, 128], P('tensor', 'fsdp'), may hold values from -0.1875 to 0.1875
- down_weight: bfloat16 [256, 8, 128, 128], P('tensor', 'fsdp'), may hold values from -0.09375 to 0.09375
- up_index: int32 [256, 8], P('tensor'), may hold values from 0 to 63, all different within a row
- down_index: int32 [256, 8], P('tensor'), may hold values from 0 to 63, all different within a row
Outputs:
- mixed: bfloat16 [768, 8192], P(('fsdp', 'tensor'))
- input_grad: bfloat16 [768, 8192], P(('fsdp', 'tensor'))
- up_grad: float32 [256, 8, 128, 128], P('tensor', 'fsdp')
- down_grad: float32 [256, 8, 128, 128], P('tensor', 'fsdp')
Inputs may be any that keep to these rules, and one draw needn't show every extreme that they name: Each row of up_index names 8 different input blocks; every block is named somewhere. Each row of down_index names 8 different output blocks; every block is named somewhere.
All inputs are finite; a program needn't handle non-finite values.
Results may differ from a plain program's by a relative error of at most 0.024.
Values may be sent and summed in bfloat16 or wider, within the bound.
No kernel may reach another device: no remote copies, remote signals or barrier semaphores. Data moves between devices by JAX's collectives and lax.ppermute only.
A program may use at most 192 MiB of HBM per device.

v0:
```python
import functools

import jax
import jax.numpy as jnp
from jax import lax
from jax.experimental import pallas as pl
from jax.experimental.pallas import tpu as pltpu
from jax.sharding import PartitionSpec as P

BLK = 128
CHUNKS = 4
MIB = 1 << 20
US = 3.69e6
NT = (((1,), (1,)), ((), ()))
TN = (((0,), (0,)), ((), ()))


def dot(a, b, dims=(((1,), (0,)), ((), ()))):
    return lax.dot_general(a, b, dims, preferred_element_type=jnp.float32)


def columns(ref, blocks, offset=0):
    parts = [ref[:, pl.ds(pl.multiple_of(b * BLK + offset, BLK), BLK)] for b in blocks]
    return parts[0] if len(parts) == 1 else jnp.concatenate(parts, axis=1)


def side_by_side(ref, j, slots):
    parts = [ref[j, s] for s in range(slots)]
    return parts[0] if len(parts) == 1 else jnp.concatenate(parts, axis=1)


def hidden_pair(n, j, jj, me, up_idx, down_idx, rows, ups, downs):
    slots = ups[0].shape[1]
    width = rows.shape[1] // 2
    pre = jnp.zeros((rows.shape[0], BLK), jnp.float32)
    grad = jnp.zeros((rows.shape[0], BLK), jnp.float32)
    for r in range(n):
        k = (me ^ r) * slots
        chosen = columns(rows, [up_idx[j, k + s] for s in range(slots)])
        pre = pre + dot(chosen, ups[r][jj].reshape(slots * BLK, BLK))
        picked = columns(rows, [down_idx[j, k + s] for s in range(slots)], width)
        grad = grad + dot(picked, side_by_side(downs[r], jj, slots), NT)
    sigma = jax.nn.sigmoid(pre)
    hidden = (pre * sigma).astype(jnp.bfloat16)
    return hidden, (grad * sigma * (1.0 + pre * (1.0 - sigma))).astype(jnp.bfloat16)


def add_spread(n, j, jj, me, idx, h, ws, total, offset, which):
    slots = ws[0].shape[1]
    for r in range(n):
        k = (me ^ r) * slots
        if which == 0:
            terms = dot(h, side_by_side(ws[r], jj, slots))
        else:
            terms = dot(h, ws[r][jj].reshape(slots * BLK, BLK), NT)
        for s in range(slots):
            at = pl.ds(pl.multiple_of(idx[j, k + s] * BLK + offset, BLK), BLK)
            total[:, at] += terms[:, s * BLK : (s + 1) * BLK]


def forward_kernel(n, firsts, resumed, me_ref, up_idx, down_idx, rows, *refs):
    groups = len(firsts)
    if resumed:
        partial, refs = refs[0], refs[1:]
    ups = [refs[2 * n * g : 2 * n * g + n] for g in range(groups)]
    downs = [refs[2 * n * g + n : 2 * n * (g + 1)] for g in range(groups)]
    hs, out_ref = refs[2 * n * groups : (2 * n + 1) * groups], refs[(2 * n + 1) * groups]
    total = refs[-2] if resumed else out_ref
    per_step = ups[0][0].shape[0]
    width = rows.shape[1] // 2
    step = pl.program_id(0)
    me = me_ref[0]
    if resumed:
        copy = pltpu.make_async_copy(partial, total, refs[-1])

    @pl.when(step == 0)
    def _():
        if resumed:
            copy.start()
        else:

            @pl.loop(0, total.shape[0] // 16)
            def _(i):
                at = pl.ds(pl.multiple_of(i * 16, 16), 16)
                total[at] = jnp.zeros((16, total.shape[1]), total.dtype)

    blocks = [(g, jj) for g in range(groups) for jj in range(per_step)]
    for g, jj in blocks:
        j = firsts[g] + step * per_step + jj
        hidden, pre_grad = hidden_pair(n, j, jj, me, up_idx, down_idx, rows, ups[g], downs[g])
        hs[g][0, jj] = hidden
        hs[g][1, jj] = pre_grad

    if resumed:

        @pl.when(step == 0)
        def _():
            copy.wait()

    for g, jj in blocks:
        j = firsts[g] + step * per_step + jj
        add_spread(n, j, jj, me, down_idx, hs[g][0, jj], downs[g], total, 0, 0)
        add_spread(n, j, jj, me, up_idx, hs[g][1, jj], ups[g], total, width, 1)

    if resumed:

        @pl.when(step == pl.num_programs(0) - 1)
        def _():
            @pl.loop(0, total.shape[0] // 16)
            def _(i):
                at = pl.ds(pl.multiple_of(i * 16, 16), 16)
                out_ref[at] = total[at].astype(out_ref.dtype)


def grad_kernel(n, first, per_step, half, me_ref, up_idx, down_idx, mine_hbm, other_hbm, h_mine, *refs):
    ups, downs, outs = refs[:n], refs[n : 2 * n], refs[2 * n : -4]
    mine, other, h_other, sems = refs[-4:]
    slots = ups[0].shape[1]
    width = mine.shape[1] // 2
    me = me_ref[0]
    step = pl.program_id(0)
    copies = [
        pltpu.make_async_copy(src.at[:, pl.ds(p * width, width)], dst.at[:, pl.ds(p * width, width)], sems.at[i])
        for i, (src, dst, p) in enumerate(
            ((other_hbm, other, 0), (other_hbm, other, 1), (mine_hbm, mine, 0), (mine_hbm, mine, 1))
        )
    ]

    @pl.when(step == 0)
    def _():
        for copy in copies:
            copy.start()
        copies[0].wait()
        copies[1].wait()

    @pl.when(step == half)
    def _():
        copies[2].wait()
        copies[3].wait()

    @pl.when(step < half)
    def _():
        for jj in range(per_step):
            at = step * per_step + jj
            hidden, pre_grad = hidden_pair(
                n, first + at, jj, me, up_idx, down_idx, other, ups, downs
            )
            h_other[0, at] = hidden
            h_other[1, at] = pre_grad

    @pl.when(step >= half)
    def _():
        for jj in range(per_step):
            at = (step - half) * per_step + jj
            j = first + at
            for e, r in enumerate(range(0, n, 2)):
                k = (me ^ r) * slots
                up_cols = [up_idx[j, k + s] for s in range(slots)]
                down_cols = [down_idx[j, k + s] for s in range(slots)]
                up = dot(columns(mine, up_cols), h_mine[1, jj], TN)
                up = up + dot(columns(other, up_cols), h_other[1, at], TN)
                down = dot(h_mine[0, jj], columns(mine, down_cols, width), TN)
                down = down + dot(h_other[0, at], columns(other, down_cols, width), TN)
                for s in range(slots):
                    up_tile = up[s * BLK : (s + 1) * BLK]
                    down_tile = down[:, s * BLK : (s + 1) * BLK]
                    if e == 0:
                        outs[0][jj, s] = up_tile
                        outs[1][jj, s] = down_tile
                    else:
                        outs[1 + e][0, jj, s] = up_tile.astype(jnp.bfloat16)
                        outs[1 + e][1, jj, s] = down_tile.astype(jnp.bfloat16)


def finish_kernel(count, own_up, own_down, *refs):
    up_ref, down_ref = refs[-2:]
    up, down = own_up[...], own_down[...]
    for got in refs[:count]:
        up = up + got[0].astype(jnp.float32)
        down = down + got[1].astype(jnp.float32)
    up_ref[...] = up
    down_ref[...] = down


def smem():
    return pl.BlockSpec(memory_space=pltpu.SMEM)


def whole(shape):
    return pl.BlockSpec(shape, lambda i: (0,) * len(shape), pipeline_mode=pl.Buffered(1))


def params():
    return pltpu.CompilerParams(vmem_limit_bytes=60 * MIB)


def tiles(piece, per_step, index):
    array, lead = piece
    slots = array.shape[-3]
    if lead is None:
        return pl.BlockSpec((per_step, slots, BLK, BLK), lambda i: (index(i), 0, 0, 0))
    return pl.BlockSpec((None, per_step, slots, BLK, BLK), lambda i: (lead, index(i), 0, 0, 0))


def forward(n, first, per_group, me, up_index, down_index, rows, ups, downs, partial=None):
    resumed = partial is not None
    count = rows.shape[0]
    per_step = min(4, per_group)
    h_spec = pl.BlockSpec((2, per_step, count, BLK), lambda i: (0, i, 0, 0))
    h_shape = jax.ShapeDtypeStruct((2, per_group, count, BLK), jnp.bfloat16)
    total = jax.ShapeDtypeStruct(rows.shape, jnp.bfloat16 if resumed else jnp.float32)
    scratch = [pltpu.VMEM(rows.shape, jnp.float32), pltpu.SemaphoreType.DMA]
    pieces = ups + downs
    return pl.pallas_call(
        functools.partial(forward_kernel, n, [first], resumed),
        grid=(per_group // per_step,),
        in_specs=[smem()] * 3
        + [whole(rows.shape)]
        + [pl.BlockSpec(memory_space=pl.ANY)] * resumed
        + [tiles(piece, per_step, lambda i: i) for piece in pieces],
        out_specs=[h_spec, whole(rows.shape)],
        out_shape=[h_shape, total],
        scratch_shapes=scratch * resumed,
        compiler_params=params(),
        cost_estimate=pl.CostEstimate(flops=0, bytes_accessed=int(20 * US), transcendentals=0),
        name="forward_last" if resumed else "forward_first",
    )(
        me,
        up_index,
        down_index,
        rows,
        *([partial] if resumed else []),
        *[array for array, _ in pieces],
    )


def grads(n, start, at, per_chunk, me, up_index, down_index, mine, other, h_mine, ups, downs):
    slots = ups[0][0].shape[-3]
    count = h_mine.shape[2]
    per_step = min(4, per_chunk)
    skip = at // per_step
    half = per_chunk // per_step

    def early(i):
        return jnp.minimum(i, half - 1)

    def late(i):
        return jnp.maximum(i - half, 0)

    h_spec = pl.BlockSpec((2, per_step, count, BLK), lambda i: (0, skip + late(i), 0, 0))
    pieces = ups + downs
    w_specs = [tiles(piece, per_step, lambda i: skip + early(i)) for piece in pieces]
    own = pl.BlockSpec((per_step, slots, BLK, BLK), lambda i: (late(i), 0, 0, 0))
    sent = pl.BlockSpec((2, per_step, slots, BLK, BLK), lambda i: (0, late(i), 0, 0, 0))
    own_shape = jax.ShapeDtypeStruct((per_chunk, slots, BLK, BLK), jnp.float32)
    sent_shape = jax.ShapeDtypeStruct((2, per_chunk, slots, BLK, BLK), jnp.bfloat16)
    return pl.pallas_call(
        functools.partial(grad_kernel, n, start + at, per_step, half),
        grid=(2 * half,),
        in_specs=[smem()] * 3 + [pl.BlockSpec(memory_space=pl.ANY)] * 2 + [h_spec] + w_specs,
        out_specs=[own] * 2 + [sent] * (n // 2 - 1),
        out_shape=[own_shape] * 2 + [sent_shape] * (n // 2 - 1),
        scratch_shapes=[
            pltpu.VMEM(mine.shape, mine.dtype),
            pltpu.VMEM(mine.shape, mine.dtype),
            pltpu.VMEM((2, per_chunk, count, BLK), jnp.bfloat16),
            pltpu.SemaphoreType.DMA((4,)),
        ],
        compiler_params=params(),
        cost_estimate=pl.CostEstimate(flops=0, bytes_accessed=int(12 * US), transcendentals=0),
        name="grad_chunk",
    )(me, up_index, down_index, mine, other, h_mine, *[array for array, _ in pieces])


def finish(first, blocks, up, down, got, done):
    per_chunk, slots = up.shape[:2]
    per_step = 4
    at = first // per_step
    own = pl.BlockSpec((per_step, slots, BLK, BLK), lambda i: (i, 0, 0, 0))
    sent = pl.BlockSpec((2, per_step, slots, BLK, BLK), lambda i: (0, i, 0, 0, 0))
    part = pl.BlockSpec((per_step, slots, BLK, BLK), lambda i: (at + i, 0, 0, 0))
    kept = pl.BlockSpec(memory_space=pl.ANY)
    shape = jax.ShapeDtypeStruct((blocks, slots, BLK, BLK), jnp.float32)
    return pl.pallas_call(
        functools.partial(finish_kernel, len(got)),
        grid=(per_chunk // per_step,),
        in_specs=[own] * 2 + [sent] * len(got) + [kept] * len(done),
        out_specs=[part] * 2,
        out_shape=[shape] * 2,
        input_output_aliases={2 + len(got) + i: i for i in range(len(done))},
        compiler_params=params(),
        cost_estimate=pl.CostEstimate(flops=0, bytes_accessed=int(3 * US), transcendentals=0),
        name="finish_chunk",
    )(up, down, *got, *done)


def after(a, *earlier):
    return lax.optimization_barrier((a,) + earlier)[0]


def exchange(a, bit, n):
    return lax.ppermute(a, "fsdp", [(i, i ^ bit) for i in range(n)])


def gather(n, up, down, late=()):
    bits = [1 << b for b in range(n.bit_length() - 1)]
    first, last = bits[0], bits[-1]
    ups = {0: up, first: exchange(up, first, n), last: exchange(up, last, n)}
    downs = {0: down, first: exchange(down, first, n), last: exchange(down, last, n)}
    marks = [ups[first], downs[last], ups[last], downs[first]]
    for held, order in ((ups, bits[1:]), (downs, bits[-2::-1])):
        for bit in order:
            for r in list(held):
                if r ^ bit not in held:
                    a = after(held[r], *marks, *late) if late else held[r]
                    held[r ^ bit] = exchange(a, bit, n)
    return [(ups[r], None) for r in range(n)], [(downs[r], None) for r in range(n)], marks


def body(n, tokens, out_grad, up_weight, down_weight, up_index, down_index):
    width = tokens.shape[1]
    blocks = up_weight.shape[0]
    per_chunk, per_group = blocks // CHUNKS, blocks // 2
    me = lax.axis_index("fsdp").astype(jnp.int32).reshape(1)

    both = jnp.concatenate([tokens, out_grad], axis=1)
    mine = lax.all_gather(both, "tensor", axis=0, tiled=True)
    swapped = exchange(both, 1, n)

    def forward_group(g, rows, *partial):
        return forward(
            n, g * per_group, per_group, me, up_index, down_index, rows, ups[g], downs[g], *partial
        )

    up, down, marks = gather(n, up_weight[:per_group], down_weight[:per_group])
    other = lax.all_gather(after(swapped, *marks), "tensor", axis=0, tiled=True)
    ups, downs = [up], [down]
    h, partial = forward_group(0, mine)
    hs = [h]
    ends = (up[-1][0], down[-1][0])
    up, down = after(up_weight[per_group:], *ends), after(down_weight[per_group:], *ends)
    up, down, marks = gather(n, up, down, (h,))
    ups.append(up)
    downs.append(down)

    def grad_chunk(c, *earlier):
        g, at = c * per_chunk // per_group, c * per_chunk % per_group
        rows = after(other, *earlier)
        up, down, *sent = grads(
            n, g * per_group, at, per_chunk, me, up_index, down_index, mine, rows, hs[g], ups[g], downs[g]
        )
        return up, down, sent, [exchange(part, 2 * (e + 1), n) for e, part in enumerate(sent)]

    parts = [grad_chunk(0, *marks)]
    h, total = forward_group(1, after(mine, *parts[0][2]), partial)
    hs.append(h)
    sums = lax.psum_scatter(after(total, *parts[0][3]), "tensor", scatter_dimension=0, tiled=True)
    for c in range(1, CHUNKS):
        parts.append(grad_chunk(c, total, *parts[c - 1][2]))

    grad_out = ()
    for c, (up, down, _, got) in enumerate(parts):
        grad_out = finish(c * per_chunk, blocks, up, down, got, grad_out)
    return (sums[:, :width], sums[:, width:], *grad_out)


def solution(mesh):
    return jax.shard_map(
        functools.partial(body, mesh.shape["fsdp"]),
        mesh=mesh,
        in_specs=(
            P(("fsdp", "tensor"), None),
            P(("fsdp", "tensor"), None),
            P("tensor", "fsdp", None, None),
            P("tensor", "fsdp", None, None),
            P("tensor", None),
            P("tensor", None),
        ),
        out_specs=(
            P(("fsdp", "tensor"), None),
            P(("fsdp", "tensor"), None),
            P("tensor", "fsdp", None, None),
            P("tensor", "fsdp", None, None),
        ),
        check_vma=False,
    )
```

profile of v0, /device:TPU:0, one launch (start us, length us, event | category | flops | bytes accessed | tf_op | source)
XLA Modules:
  0.0 286.5 jit_solution(13680694209864057478)
XLA Ops:
  8.2 1.0 constant_dynamic-update-slice_fusion
  10.3 1.8 fusion.1
  12.1 3.0 %collective-permute-start.3 = (bf16[16,2,128,128]{3,2,1,0:T(8,128)(2,1)S(1)}, bf16[16,2,128,128]{3,2,1,0:T(8,128)(2,1)}, u32[]{:S(2)}, u32[]{:S(2)}) collective-permute-start(bf16[16,2,128,128]{3,2,1,0:T(8,128)(2,1)S(1)} %get-tuple-element.77.refs_0_), channel_id=1, source_target_pairs={{0,16},{8,24},{16,0},{24,8},{1,17},{9,25},{17,1},{25,9},{2,18},{10... | collective-permute-start | bytes 3145736 | tf_op jit(solution)/shard_map/ppermute | solution.py:302
  15.2 1.5 collective-permute-start.1
  16.7 1.1 fusion
  18.4 1.9 collective-permute-start
  20.3 58.9 %collective-permute-done = bf16[24,16384]{1,0:T(8,128)(2,1)} collective-permute-done((bf16[24,16384]{1,0:T(8,128)(2,1)S(1)}, bf16[24,16384]{1,0:T(8,128)(2,1)}, u32[]{:S(2)}, u32[]{:S(2)}) %collective-permute-start) | collective-permute-done | bytes 786464 | tf_op jit(solution)/shard_map/ppermute | solution.py:302
  79.7 1.6 collective-permute-start.6
  81.4 21.9 %collective-permute-done.5.refs_3_ = bf16[16,2,128,128]{3,2,1,0:T(8,128)(2,1)S(1)} collective-permute-done((bf16[16,2,128,128]{3,2,1,0:T(8,128)(2,1)}, bf16[16,2,128,128]{3,2,1,0:T(8,128)(2,1)S(1)}, u32[]{:S(2)}, u32[]{:S(2)}) %collective-permute-start.5) | collective-permute-done | bytes 1048608 | tf_op jit(solution)/shard_map/ppermute | solution.py:302
  103.7 1.3 collective-permute-start.9
  105.0 1.5 collective-permute-start.7
  109.1 20.5 %forward_first.1 = (bf16[2,16,192,128]{3,2,1,0:T(8,128)(2,1)}, f32[192,16384]{1,0:T(8,128)}) custom-call(s32[1]{0:T(128)} %bitcast.me_ref, s32[32,8]{1,0:T(8,128)} %copy.20.up_idx, s32[32,8]{1,0:T(8,128)} %copy.21.down_idx, bf16[192,16384]{1,0:T(8,128)(2,1)} %all-gather.3.cloned.1.call-done.rows.mine_hbm, bf16[16,2,128,128]{3,2,1,0:T(8,128)(2,1)} %copy-done.2, ...), custom_call_target="tpu_custom_call" | custom-call | bytes 73800000 | tf_op jit(solution)/shard_map/forward_first/pallas_call | solution.py:214
  129.9 1.3 collective-permute-done.7.refs_2_.refs_1_
  131.2 18.7 %collective-permute-done.10.refs_6_.refs_5_ = bf16[16,2,128,128]{3,2,1,0:T(8,128)(2,1)} collective-permute-done((bf16[16,2,128,128]{3,2,1,0:T(8,128)(2,1)S(1)}, bf16[16,2,128,128]{3,2,1,0:T(8,128)(2,1)}, u32[]{:S(2)}, u32[]{:S(2)}) %collective-permute-start.10) | collective-permute-done | bytes 1048608 | tf_op jit(solution)/shard_map/ppermute | solution.py:302
  150.9 1.1 collective-permute-start.12
  152.1 10.7 %grad_chunk.4 = (f32[8,2,128,128]{3,2,1,0:T(8,128)}, f32[8,2,128,128]{3,2,1,0:T(8,128)}, bf16[2,8,2,128,128]{4,3,2,1,0:T(8,128)(2,1)}) custom-call(s32[1]{0:T(128)} %bitcast.me_ref, s32[32,8]{1,0:T(8,128)} %copy.20.up_idx, s32[32,8]{1,0:T(8,128)} %copy.21.down_idx, bf16[192,16384]{1,0:T(8,128)(2,1)} %all-gather.3.cloned.1.call-done.rows.mine_hbm, ...), custom_call_target="tpu_custom_call" | custom-call | bytes 44280000 | tf_op jit(solution)/shard_map/grad_chunk/pallas_call | solution.py:257
  162.8 1.7 collective-permute-start.13
  164.5 11.8 %collective-permute-done.11.refs_4_.refs_3_ = bf16[16,2,128,128]{3,2,1,0:T(8,128)(2,1)S(1)} collective-permute-done((bf16[16,2,128,128]{3,2,1,0:T(8,128)(2,1)}, bf16[16,2,128,128]{3,2,1,0:T(8,128)(2,1)S(1)}, u32[]{:S(2)}, u32[]{:S(2)}) %collective-permute-start.11) | collective-permute-done | bytes 1048608 | tf_op jit(solution)/shard_map/ppermute | solution.py:302
  177.6 23.7 %forward_last.1 = (bf16[2,16,192,128]{3,2,1,0:T(8,128)(2,1)}, bf16[192,16384]{1,0:T(8,128)(2,1)}) custom-call(s32[1]{0:T(128)} %bitcast.me_ref, s32[32,8]{1,0:T(8,128)} %copy.20.up_idx, s32[32,8]{1,0:T(8,128)} %copy.21.down_idx, bf16[192,16384]{1,0:T(8,128)(2,1)} %all-gather.3.cloned.1.call-done.rows.mine_hbm, f32[192,16384]{1,0:T(8,128)} %get-tuple-element.46.refs_0_, ...), custom_call_target="tpu_custom_call" | custom-call | bytes 73800000 | tf_op jit(solution)/shard_map/forward_last/pallas_call | solution.py:214
  201.4 11.0 %grad_chunk.5 = (f32[8,2,128,128]{3,2,1,0:T(8,128)}, f32[8,2,128,128]{3,2,1,0:T(8,128)}, bf16[2,8,2,128,128]{4,3,2,1,0:T(8,128)(2,1)}) custom-call(s32[1]{0:T(128)} %bitcast.me_ref, s32[32,8]{1,0:T(8,128)} %copy.20.up_idx, s32[32,8]{1,0:T(8,128)} %copy.21.down_idx, bf16[192,16384]{1,0:T(8,128)(2,1)} %all-gather.3.cloned.1.call-done.rows.mine_hbm, ...), custom_call_target="tpu_custom_call" | custom-call | bytes 44280000 | tf_op jit(solution)/shard_map/grad_chunk/pallas_call | solution.py:257
  212.4 1.1 collective-permute-start.16
  213.4 11.0 %grad_chunk.6 = (f32[8,2,128,128]{3,2,1,0:T(8,128)}, f32[8,2,128,128]{3,2,1,0:T(8,128)}, bf16[2,8,2,128,128]{4,3,2,1,0:T(8,128)(2,1)}) custom-call(s32[1]{0:T(128)} %bitcast.me_ref, s32[32,8]{1,0:T(8,128)} %copy.20.up_idx, s32[32,8]{1,0:T(8,128)} %copy.21.down_idx, bf16[192,16384]{1,0:T(8,128)(2,1)} %all-gather.3.cloned.1.call-done.rows.mine_hbm, ...), custom_call_target="tpu_custom_call" | custom-call | bytes 44280000 | tf_op jit(solution)/shard_map/grad_chunk/pallas_call | solution.py:257
  224.5 1.1 collective-permute-start.15
  225.5 10.8 %grad_chunk.7 = (f32[8,2,128,128]{3,2,1,0:T(8,128)}, f32[8,2,128,128]{3,2,1,0:T(8,128)}, bf16[2,8,2,128,128]{4,3,2,1,0:T(8,128)(2,1)}) custom-call(s32[1]{0:T(128)} %bitcast.me_ref, s32[32,8]{1,0:T(8,128)} %copy.20.up_idx, s32[32,8]{1,0:T(8,128)} %copy.21.down_idx, bf16[192,16384]{1,0:T(8,128)(2,1)} %all-gather.3.cloned.1.call-done.rows.mine_hbm, ...), custom_call_target="tpu_custom_call" | custom-call | bytes 44280000 | tf_op jit(solution)/shard_map/grad_chunk/pallas_call | solution.py:257
  236.3 1.1 collective-permute-start.14
  237.5 2.9 %finish_chunk.4 = (f32[32,2,128,128]{3,2,1,0:T(8,128)}, f32[32,2,128,128]{3,2,1,0:T(8,128)}) custom-call(f32[8,2,128,128]{3,2,1,0:T(8,128)} %get-tuple-element.64.own_up, f32[8,2,128,128]{3,2,1,0:T(8,128)} %get-tuple-element.65.own_down, bf16[2,8,2,128,128]{4,3,2,1,0:T(8,128)(2,1)} %copy-done.10), custom_call_target="tpu_custom_call" | custom-call | bytes 11070000 | tf_op jit(solution)/shard_map/finish_chunk/pallas_call | solution.py:284
  241.4 3.0 %finish_chunk.5 = (f32[32,2,128,128]{3,2,1,0:T(8,128)}, f32[32,2,128,128]{3,2,1,0:T(8,128)}) custom-call(f32[8,2,128,128]{3,2,1,0:T(8,128)} %get-tuple-element.62.own_up, f32[8,2,128,128]{3,2,1,0:T(8,128)} %get-tuple-element.63.own_down, bf16[2,8,2,128,128]{4,3,2,1,0:T(8,128)(2,1)} %copy-done.12, ...), custom_call_target="tpu_custom_call", output_to_operand_aliasing={{0}: (3, {}), {1}: (4, {})} | custom-call | bytes 11070000 | tf_op jit(solution)/shard_map/finish_chunk/pallas_call | solution.py:284
  244.3 16.9 %collective-permute-done.15.refs_0_ = bf16[2,8,2,128,128]{4,3,2,1,0:T(8,128)(2,1)S(1)} collective-permute-done((bf16[2,8,2,128,128]{4,3,2,1,0:T(8,128)(2,1)}, bf16[2,8,2,128,128]{4,3,2,1,0:T(8,128)(2,1)S(1)}, u32[]{:S(2)}, u32[]{:S(2)}) %collective-permute-start.15) | collective-permute-done | bytes 1048608 | tf_op jit(solution)/shard_map/ppermute | solution.py:302
  262.2 2.9 %finish_chunk.6 = (f32[32,2,128,128]{3,2,1,0:T(8,128)}, f32[32,2,128,128]{3,2,1,0:T(8,128)}) custom-call(f32[8,2,128,128]{3,2,1,0:T(8,128)} %get-tuple-element.60.own_up, f32[8,2,128,128]{3,2,1,0:T(8,128)} %get-tuple-element.61.own_down, bf16[2,8,2,128,128]{4,3,2,1,0:T(8,128)(2,1)} %copy-done.11, ...), custom_call_target="tpu_custom_call", output_to_operand_aliasing={{0}: (3, {}), {1}: (4, {})} | custom-call | bytes 11070000 | tf_op jit(solution)/shard_map/finish_chunk/pallas_call | solution.py:284
  265.1 9.0 %collective-permute-done.14.refs_0_ = bf16[2,8,2,128,128]{4,3,2,1,0:T(8,128)(2,1)S(1)} collective-permute-done((bf16[2,8,2,128,128]{4,3,2,1,0:T(8,128)(2,1)}, bf16[2,8,2,128,128]{4,3,2,1,0:T(8,128)(2,1)S(1)}, u32[]{:S(2)}, u32[]{:S(2)}) %collective-permute-start.14) | collective-permute-done | bytes 1048608 | tf_op jit(solution)/shard_map/ppermute | solution.py:302
  275.1 2.9 %finish_chunk.7 = (f32[32,2,128,128]{3,2,1,0:T(8,128)}, f32[32,2,128,128]{3,2,1,0:T(8,128)}) custom-call(f32[8,2,128,128]{3,2,1,0:T(8,128)} %get-tuple-element.57.own_up, f32[8,2,128,128]{3,2,1,0:T(8,128)} %get-tuple-element.58.own_down, bf16[2,8,2,128,128]{4,3,2,1,0:T(8,128)(2,1)} %copy-done.13, ...), custom_call_target="tpu_custom_call", output_to_operand_aliasing={{0}: (3, {}), {1}: (4, {})} | custom-call | bytes 11070000 | tf_op jit(solution)/shard_map/finish_chunk/pallas_call | solution.py:284
  278.0 2.0 fusion.2
  (60 shorter events, 11.7 us)
Async XLA Ops:
  7.2 101.9 %all-gather.3.cloned.1.call-start = ((), (), s32[]{:S(2)}) async-start(), calls=%async_computation.1 | async-start | bytes 7077888 | tf_op jit(solution)/shard_map/all_gather | solution.py:327
  10.2 97.6 %copy-start.14 = (s32[32,8]{0,1:T(8,128)S(1)}, s32[32,8]{0,1:T(8,128)}, u32[]{:S(2)}) copy-start(s32[32,8]{0,1:T(8,128)} %param.10) | copy-start | bytes 3076
  10.2 98.2 %copy-start.15 = (s32[32,8]{0,1:T(8,128)S(1)}, s32[32,8]{0,1:T(8,128)}, u32[]{:S(2)}) copy-start(s32[32,8]{0,1:T(8,128)} %param.11) | copy-start | bytes 3076
  10.2 141.9 %all-gather.5.cloned.1.call-start = ((), (), s32[]{:S(2)}) async-start(), calls=%async_computation.2 | async-start | bytes 7077888 | tf_op jit(solution)/shard_map/all_gather | solution.py:336
  10.2 6.4 %copy-start.7 = (bf16[32,2,128,128]{3,2,1,0:T(8,128)(2,1)S(1)}, bf16[32,2,128,128]{3,2,1,0:T(8,128)(2,1)}, u32[]{:S(2)}) copy-start(bf16[32,2,128,128]{3,2,1,0:T(8,128)(2,1)} %param.9) | copy-start | bytes 6291460
  10.3 8.1 %copy-start.9 = (bf16[24,16384]{1,0:T(8,128)(2,1)S(1)}, bf16[24,16384]{1,0:T(8,128)(2,1)}, u32[]{:S(2)}) copy-start(bf16[24,16384]{1,0:T(8,128)(2,1)} %copy-done.8) | copy-start | bytes 2359300
  12.1 97.0 %copy-start.2 = (bf16[16,2,128,128]{3,2,1,0:T(8,128)(2,1)}, bf16[16,2,128,128]{3,2,1,0:T(8,128)(2,1)S(1)}, u32[]{:S(2)}) copy-start(bf16[16,2,128,128]{3,2,1,0:T(8,128)(2,1)S(1)} %get-tuple-element.77.refs_0_) | copy-start | bytes 3145732
  12.1 117.6 %copy-start = (bf16[16,2,128,128]{3,2,1,0:T(8,128)(2,1)}, bf16[16,2,128,128]{3,2,1,0:T(8,128)(2,1)S(1)}, u32[]{:S(2)}) copy-start(bf16[16,2,128,128]{3,2,1,0:T(8,128)(2,1)S(1)} %get-tuple-element.40.refs_1_.refs_0_) | copy-start | bytes 3145732
  12.1 67.1 %collective-permute-start.3 = (bf16[16,2,128,128]{3,2,1,0:T(8,128)(2,1)S(1)}, bf16[16,2,128,128]{3,2,1,0:T(8,128)(2,1)}, u32[]{:S(2)}, u32[]{:S(2)}) collective-permute-start(bf16[16,2,128,128]{3,2,1,0:T(8,128)(2,1)S(1)} %get-tuple-element.77.refs_0_), channel_id=1, source_target_pairs={{0,16},{8,24},{16,0},{24,8},{1,17},{9,25},{17,1},{25,9},{2,18},{10... | collective-permute-start | bytes 3145736 | tf_op jit(solution)/shard_map/ppermute | solution.py:302
  15.2 64.1 %collective-permute-start.1 = (bf16[16,2,128,128]{3,2,1,0:T(8,128)(2,1)S(1)}, bf16[16,2,128,128]{3,2,1,0:T(8,128)(2,1)}, u32[]{:S(2)}, u32[]{:S(2)}) collective-permute-start(bf16[16,2,128,128]{3,2,1,0:T(8,128)(2,1)S(1)} %get-tuple-element.77.refs_0_), channel_id=1, source_target_pairs={{0,8},{8,0},{16,24},{24,16},{1,9},{9,1},{17,25},{25,17},{2,10},{10... | collective-permute-start | bytes 3145736 | tf_op jit(solution)/shard_map/ppermute | solution.py:302
  17.8 111.9 %copy-start.1 = (bf16[16,2,128,128]{3,2,1,0:T(8,128)(2,1)}, bf16[16,2,128,128]{3,2,1,0:T(8,128)(2,1)S(1)}, u32[]{:S(2)}) copy-start(bf16[16,2,128,128]{3,2,1,0:T(8,128)(2,1)S(1)} %get-tuple-element.41.refs_5_.refs_4_) | copy-start | bytes 3145732
  17.8 61.4 %collective-permute-start.4 = (bf16[16,2,128,128]{3,2,1,0:T(8,128)(2,1)}, bf16[16,2,128,128]{3,2,1,0:T(8,128)(2,1)}, u32[]{:S(2)}, u32[]{:S(2)}) collective-permute-start(bf16[16,2,128,128]{3,2,1,0:T(8,128)(2,1)} %get-tuple-element.75.refs_4_), channel_id=1, source_target_pairs={{0,8},{8,0},{16,24},{24,16},{1,9},{9,1},{17,25},{25,17},{2,10},{10... | collective-permute-start | bytes 3145736 | tf_op jit(solution)/shard_map/ppermute | solution.py:302
  18.3 60.9 %collective-permute-start.2 = (bf16[16,2,128,128]{3,2,1,0:T(8,128)(2,1)}, bf16[16,2,128,128]{3,2,1,0:T(8,128)(2,1)}, u32[]{:S(2)}, u32[]{:S(2)}) collective-permute-start(bf16[16,2,128,128]{3,2,1,0:T(8,128)(2,1)} %get-tuple-element.75.refs_4_), channel_id=1, source_target_pairs={{0,16},{8,24},{16,0},{24,8},{1,17},{9,25},{17,1},{25,9},{2,18},{10... | collective-permute-start | bytes 3145736 | tf_op jit(solution)/shard_map/ppermute | solution.py:302
  18.4 60.8 %collective-permute-start = (bf16[24,16384]{1,0:T(8,128)(2,1)S(1)}, bf16[24,16384]{1,0:T(8,128)(2,1)}, u32[]{:S(2)}, u32[]{:S(2)}) collective-permute-start(bf16[24,16384]{1,0:T(8,128)(2,1)S(1)} %copy-done.9), channel_id=1, source_target_pairs={{0,8},{8,0},{16,24},{24,16},{1,9},{9,1},{17,25},{25,17},{2,10},{10... | collective-permute-start | bytes 2359304 | tf_op jit(solution)/shard_map/ppermute | solution.py:302
  79.3 198.7 %reduce-scatter.2.cloned.1.call-start = ((), (), s32[]{:S(2)}) async-start(), calls=%async_computation.3 | async-start | bytes 7077888 | tf_op jit(solution)/shard_map/reduce_scatter | solution.py:357
  79.3 24.0 %collective-permute-start.5 = (bf16[16,2,128,128]{3,2,1,0:T(8,128)(2,1)}, bf16[16,2,128,128]{3,2,1,0:T(8,128)(2,1)S(1)}, u32[]{:S(2)}, u32[]{:S(2)}) collective-permute-start(bf16[16,2,128,128]{3,2,1,0:T(8,128)(2,1)} %collective-permute-done.1.refs_1_), channel_id=1, source_target_pairs={{0,16},{8,24},{16,0},{24,8},{1,17},{9,25},{17,1},{25,9},{2,18},{10... | collective-permute-start | bytes 3145736 | tf_op jit(solution)/shard_map/ppermute | solution.py:302
  79.7 24.0 %collective-permute-start.6 = (bf16[16,2,128,128]{3,2,1,0:T(8,128)(2,1)}, bf16[16,2,128,128]{3,2,1,0:T(8,128)(2,1)S(1)}, u32[]{:S(2)}, u32[]{:S(2)}) collective-permute-start(bf16[16,2,128,128]{3,2,1,0:T(8,128)(2,1)} %collective-permute-done.2.refs_6_), channel_id=1, source_target_pairs={{0,8},{8,0},{16,24},{24,16},{1,9},{9,1},{17,25},{25,17},{2,10},{10... | collective-permute-start | bytes 3145736 | tf_op jit(solution)/shard_map/ppermute | solution.py:302
  103.3 3.2 %copy-start.3 = (bf16[16,2,128,128]{3,2,1,0:T(8,128)(2,1)}, bf16[16,2,128,128]{3,2,1,0:T(8,128)(2,1)S(1)}, u32[]{:S(2)}) copy-start(bf16[16,2,128,128]{3,2,1,0:T(8,128)(2,1)S(1)} %collective-permute-done.5.refs_3_) | copy-start | bytes 3145732
  103.7 3.4 %copy-start.4 = (bf16[16,2,128,128]{3,2,1,0:T(8,128)(2,1)}, bf16[16,2,128,128]{3,2,1,0:T(8,128)(2,1)S(1)}, u32[]{:S(2)}) copy-start(bf16[16,2,128,128]{3,2,1,0:T(8,128)(2,1)S(1)} %collective-permute-done.6.refs_7_) | copy-start | bytes 3145732
  103.7 26.2 %collective-permute-start.9 = (bf16[16,2,128,128]{3,2,1,0:T(8,128)(2,1)S(1)}, bf16[16,2,128,128]{3,2,1,0:T(8,128)(2,1)}, u32[]{:S(2)}, u32[]{:S(2)}) collective-permute-start(bf16[16,2,128,128]{3,2,1,0:T(8,128)(2,1)S(1)} %get-tuple-element.40.refs_1_.refs_0_), channel_id=1, source_target_pairs={{0,16},{8,24},{16,0},{24,8},{1,17},{9,25},{17,1},{25,9},{2,18},{10... | collective-permute-start | bytes 3145736 | tf_op jit(solution)/shard_map/ppermute | solution.py:302
  105.0 26.2 %collective-permute-start.7 = (bf16[16,2,128,128]{3,2,1,0:T(8,128)(2,1)S(1)}, bf16[16,2,128,128]{3,2,1,0:T(8,128)(2,1)}, u32[]{:S(2)}, u32[]{:S(2)}) collective-permute-start(bf16[16,2,128,128]{3,2,1,0:T(8,128)(2,1)S(1)} %get-tuple-element.40.refs_1_.refs_0_), channel_id=1, source_target_pairs={{0,8},{8,0},{16,24},{24,16},{1,9},{9,1},{17,25},{25,17},{2,10},{10... | collective-permute-start | bytes 3145736 | tf_op jit(solution)/shard_map/ppermute | solution.py:302
  106.5 43.4 %collective-permute-start.10 = (bf16[16,2,128,128]{3,2,1,0:T(8,128)(2,1)S(1)}, bf16[16,2,128,128]{3,2,1,0:T(8,128)(2,1)}, u32[]{:S(2)}, u32[]{:S(2)}) collective-permute-start(bf16[16,2,128,128]{3,2,1,0:T(8,128)(2,1)S(1)} %get-tuple-element.41.refs_5_.refs_4_), channel_id=1, source_target_pairs={{0,8},{8,0},{16,24},{24,16},{1,9},{9,1},{17,25},{25,17},{2,10},{10... | collective-permute-start | bytes 3145736 | tf_op jit(solution)/shard_map/ppermute | solution.py:302
  107.1 42.9 %collective-permute-start.8 = (bf16[16,2,128,128]{3,2,1,0:T(8,128)(2,1)S(1)}, bf16[16,2,128,128]{3,2,1,0:T(8,128)(2,1)}, u32[]{:S(2)}, u32[]{:S(2)}) collective-permute-start(bf16[16,2,128,128]{3,2,1,0:T(8,128)(2,1)S(1)} %get-tuple-element.41.refs_5_.refs_4_), channel_id=1, source_target_pairs={{0,16},{8,24},{16,0},{24,8},{1,17},{9,25},{17,1},{25,9},{2,18},{10... | collective-permute-start | bytes 3145736 | tf_op jit(solution)/shard_map/ppermute | solution.py:302
  149.9 26.3 %collective-permute-start.11 = (bf16[16,2,128,128]{3,2,1,0:T(8,128)(2,1)}, bf16[16,2,128,128]{3,2,1,0:T(8,128)(2,1)S(1)}, u32[]{:S(2)}, u32[]{:S(2)}) collective-permute-start(bf16[16,2,128,128]{3,2,1,0:T(8,128)(2,1)} %collective-permute-done.7.refs_2_.refs_1_), channel_id=1, source_target_pairs={{0,16},{8,24},{16,0},{24,8},{1,17},{9,25},{17,1},{25,9},{2,18},{10... | collective-permute-start | bytes 3145736 | tf_op jit(solution)/shard_map/ppermute | solution.py:302
  150.9 25.3 %collective-permute-start.12 = (bf16[16,2,128,128]{3,2,1,0:T(8,128)(2,1)}, bf16[16,2,128,128]{3,2,1,0:T(8,128)(2,1)S(1)}, u32[]{:S(2)}, u32[]{:S(2)}) collective-permute-start(bf16[16,2,128,128]{3,2,1,0:T(8,128)(2,1)} %collective-permute-done.8.refs_7_.refs_6_), channel_id=1, source_target_pairs={{0,8},{8,0},{16,24},{24,16},{1,9},{9,1},{17,25},{25,17},{2,10},{10... | collective-permute-start | bytes 3145736 | tf_op jit(solution)/shard_map/ppermute | solution.py:302
  162.8 38.5 %collective-permute-start.13 = (bf16[2,8,2,128,128]{4,3,2,1,0:T(8,128)(2,1)}, bf16[2,8,2,128,128]{4,3,2,1,0:T(8,128)(2,1)S(1)}, u32[]{:S(2)}, u32[]{:S(2)}) collective-permute-start(bf16[2,8,2,128,128]{4,3,2,1,0:T(8,128)(2,1)} %get-tuple-element.44), channel_id=1, source_target_pairs={{0,16},{8,24},{16,0},{24,8},{1,17},{9,25},{17,1},{25,9},{2,18},{10... | collective-permute-start | bytes 3145736 | tf_op jit(solution)/shard_map/ppermute | solution.py:302
  176.3 1.4 copy-start.6
  201.3 11.0 %copy-start.10 = (bf16[2,8,2,128,128]{4,3,2,1,0:T(8,128)(2,1)}, bf16[2,8,2,128,128]{4,3,2,1,0:T(8,128)(2,1)S(1)}, u32[]{:S(2)}) copy-start(bf16[2,8,2,128,128]{4,3,2,1,0:T(8,128)(2,1)S(1)} %collective-permute-done.13.refs_0_) | copy-start | bytes 3145732
  212.4 28.0 %collective-permute-start.16 = (bf16[2,8,2,128,128]{4,3,2,1,0:T(8,128)(2,1)}, bf16[2,8,2,128,128]{4,3,2,1,0:T(8,128)(2,1)S(1)}, u32[]{:S(2)}, u32[]{:S(2)}) collective-permute-start(bf16[2,8,2,128,128]{4,3,2,1,0:T(8,128)(2,1)} %get-tuple-element.52), channel_id=1, source_target_pairs={{0,16},{8,24},{16,0},{24,8},{1,17},{9,25},{17,1},{25,9},{2,18},{10... | collective-permute-start | bytes 3145736 | tf_op jit(solution)/shard_map/ppermute | solution.py:302
  224.5 36.7 %collective-permute-start.15 = (bf16[2,8,2,128,128]{4,3,2,1,0:T(8,128)(2,1)}, bf16[2,8,2,128,128]{4,3,2,1,0:T(8,128)(2,1)S(1)}, u32[]{:S(2)}, u32[]{:S(2)}) collective-permute-start(bf16[2,8,2,128,128]{4,3,2,1,0:T(8,128)(2,1)} %get-tuple-element.55), channel_id=1, source_target_pairs={{0,16},{8,24},{16,0},{24,8},{1,17},{9,25},{17,1},{25,9},{2,18},{10... | collective-permute-start | bytes 3145736 | tf_op jit(solution)/shard_map/ppermute | solution.py:302
  236.3 37.7 %collective-permute-start.14 = (bf16[2,8,2,128,128]{4,3,2,1,0:T(8,128)(2,1)}, bf16[2,8,2,128,128]{4,3,2,1,0:T(8,128)(2,1)S(1)}, u32[]{:S(2)}, u32[]{:S(2)}) collective-permute-start(bf16[2,8,2,128,128]{4,3,2,1,0:T(8,128)(2,1)} %get-tuple-element.59), channel_id=1, source_target_pairs={{0,16},{8,24},{16,0},{24,8},{1,17},{9,25},{17,1},{25,9},{2,18},{10... | collective-permute-start | bytes 3145736 | tf_op jit(solution)/shard_map/ppermute | solution.py:302
  274.1 1.0 copy-start.13
  (4 other events, 3.8 us)
Sparse Core Ops, SparseCore 0:
  10.3 67.4 all-gather.2
  79.4 64.9 all-gather.4
  201.5 70.2 reduce-scatter.1
where the time goes:
time: 287 us
  waiting for transfers between devices  139 us (48%)
  Pallas kernels  99.4 us (35%)
  starting transfers between devices  20.3 us (7%)
  between operations  13.9 us (5%)
  local copies, waits for them, and re-layouts  13.6 us (5%)
    ppermute x17, waiting for transfers between devices, exchange(): return lax.ppermute(a, 'fsdp', [(i, i ^ bit) for i in range(n)])  139 us
    pallas_call x2, Pallas kernels, forward(): pl.pallas_call(functools.partial(forward_kernel, n, [first], resumed), gr...  44.2 us
    pallas_call x4, Pallas kernels, grads(): pl.pallas_call(functools.partial(grad_kernel, n, start + at, per_step, ha...  43.6 us
    ppermute x17, starting transfers between devices, exchange(): return lax.ppermute(a, 'fsdp', [(i, i ^ bit) for i in range(n)])  20.2 us
    pallas_call x4, Pallas kernels, finish(): pl.pallas_call(functools.partial(finish_kernel, len(got)), grid=(per_chun...  11.7 us
    unnamed x35, local copies, waits for them, and re-layouts  7.61 us
  transfers between devices with their start and end apart: 20, of which 9 were waited for; matrix products, arithmetic and copies ran while one was open for 2% of the time, Pallas kernels for 35%

commit v1 on v0

--- a/solution.py
+++ b/solution.py
@@ -352,14 +352,16 @@
         return up, down, sent, [exchange(part, 2 * (e + 1), n) for e, part in enumerate(sent)]
 
     parts = [grad_chunk(0, *marks)]
-    h, total = forward_group(1, after(mine, *parts[0][2]), partial)
+    parts.append(grad_chunk(1, *parts[0][2]))
+    h, total = forward_group(1, after(mine, *parts[1][2]), partial)
     hs.append(h)
     sums = lax.psum_scatter(after(total, *parts[0][3]), "tensor", scatter_dimension=0, tiled=True)
-    for c in range(1, CHUNKS):
+    for c in range(2, CHUNKS):
         parts.append(grad_chunk(c, total, *parts[c - 1][2]))
 
     grad_out = ()
     for c, (up, down, _, got) in enumerate(parts):
+        up = after(up, *parts[-1][2])
         grad_out = finish(c * per_chunk, blocks, up, down, got, grad_out)
     return (sums[:, :width], sums[:, width:], *grad_out)
 

time: 287 us -> 280 us (0.976)
  waiting for transfers between devices: 139 us -> 134 us
    ppermute x17, waiting for transfers between devices: 139 us -> 132 us  [exchange(): return lax.ppermute(a, 'fsdp', [(i, i ^ bit) for i in range(n)])]
  transfers between devices with their start and end apart: 20 -> 20, of which waited for: 9 -> 10; matrix products, arithmetic and copies ran while one was open for 2% -> 2% of each run, Pallas kernels for 35% -> 35%
where the time goes in v1:
time: 280 us
  waiting for transfers between devices  134 us (48%)
  Pallas kernels  99 us (35%)
  starting transfers between devices  19.9 us (7%)
  between operations  13.9 us (5%)
  local copies, waits for them, and re-layouts  13.5 us (5%)
    ppermute x17, waiting for transfers between devices, exchange(): return lax.ppermute(a, 'fsdp', [(i, i ^ bit) for i in range(n)])  132 us
    pallas_call x2, Pallas kernels, forward(): pl.pallas_call(functools.partial(forward_kernel, n, [first], resumed), gr...  44.3 us
    pallas_call x4, Pallas kernels, grads(): pl.pallas_call(functools.partial(grad_kernel, n, start + at, per_step, ha...  43 us
    ppermute x17, starting transfers between devices, exchange(): return lax.ppermute(a, 'fsdp', [(i, i ^ bit) for i in range(n)])  19.8 us
    pallas_call x4, Pallas kernels, finish(): pl.pallas_call(functools.partial(finish_kernel, len(got)), grid=(per_chun...  11.8 us
    unnamed x35, local copies, waits for them, and re-layouts  7.55 us
  transfers between devices with their start and end apart: 20, of which 10 were waited for; matrix products, arithmetic and copies ran while one was open for 2% of the time, Pallas kernels for 35%

profile of v1, /device:TPU:0, one launch (start us, length us, event | category | flops | bytes accessed | tf_op | source)
XLA Modules:
  0.0 280.0 jit_solution(5678222958389640815)
XLA Ops:
  8.2 1.0 constant_dynamic-update-slice_fusion
  10.3 1.8 fusion.1
  12.1 3.0 %collective-permute-start.1 = (bf16[16,2,128,128]{3,2,1,0:T(8,128)(2,1)S(1)}, bf16[16,2,128,128]{3,2,1,0:T(8,128)(2,1)}, u32[]{:S(2)}, u32[]{:S(2)}) collective-permute-start(bf16[16,2,128,128]{3,2,1,0:T(8,128)(2,1)S(1)} %get-tuple-element.85.refs_0_), channel_id=1, source_target_pairs={{0,8},{8,0},{16,24},{24,16},{1,9},{9,1},{17,25},{25,17},{2,10},{10... | collective-permute-start | bytes 3145736 | tf_op jit(solution)/shard_map/ppermute | solution.py:302
  15.1 1.1 fusion
  16.2 1.5 collective-permute-start.2
  18.7 1.6 collective-permute-start
  20.3 57.4 %collective-permute-done = bf16[24,16384]{1,0:T(8,128)(2,1)} collective-permute-done((bf16[24,16384]{1,0:T(8,128)(2,1)S(1)}, bf16[24,16384]{1,0:T(8,128)(2,1)}, u32[]{:S(2)}, u32[]{:S(2)}) %collective-permute-start) | collective-permute-done | bytes 786464 | tf_op jit(solution)/shard_map/ppermute | solution.py:302
  77.8 1.8 collective-permute-start.5
  79.6 1.5 collective-permute-start.6
  81.1 21.3 %collective-permute-done.5.refs_3_ = bf16[16,2,128,128]{3,2,1,0:T(8,128)(2,1)S(1)} collective-permute-done((bf16[16,2,128,128]{3,2,1,0:T(8,128)(2,1)}, bf16[16,2,128,128]{3,2,1,0:T(8,128)(2,1)S(1)}, u32[]{:S(2)}, u32[]{:S(2)}) %collective-permute-start.5) | collective-permute-done | bytes 1048608 | tf_op jit(solution)/shard_map/ppermute | solution.py:302
  102.4 1.2 collective-permute-done.6.refs_7_
  103.6 1.5 collective-permute-start.7
  105.6 1.5 collective-permute-start.9
  109.0 20.6 %forward_first.1 = (bf16[2,16,192,128]{3,2,1,0:T(8,128)(2,1)}, f32[192,16384]{1,0:T(8,128)}) custom-call(s32[1]{0:T(128)} %bitcast.me_ref, s32[32,8]{1,0:T(8,128)} %copy.22.up_idx, s32[32,8]{1,0:T(8,128)} %copy.23.down_idx, bf16[192,16384]{1,0:T(8,128)(2,1)} %all-gather.3.cloned.1.call-done.rows.mine_hbm, bf16[16,2,128,128]{3,2,1,0:T(8,128)(2,1)} %copy-done.2, ...), custom_call_target="tpu_custom_call" | custom-call | bytes 73800000 | tf_op jit(solution)/shard_map/forward_first/pallas_call | solution.py:214
  129.8 1.5 collective-permute-done.8.refs_7_.refs_6_
  131.3 19.4 %collective-permute-done.9.refs_3_.refs_2_ = bf16[16,2,128,128]{3,2,1,0:T(8,128)(2,1)} collective-permute-done((bf16[16,2,128,128]{3,2,1,0:T(8,128)(2,1)S(1)}, bf16[16,2,128,128]{3,2,1,0:T(8,128)(2,1)}, u32[]{:S(2)}, u32[]{:S(2)}) %collective-permute-start.9) | collective-permute-done | bytes 1048608 | tf_op jit(solution)/shard_map/ppermute | solution.py:302
  151.8 10.7 %grad_chunk.4 = (f32[8,2,128,128]{3,2,1,0:T(8,128)}, f32[8,2,128,128]{3,2,1,0:T(8,128)}, bf16[2,8,2,128,128]{4,3,2,1,0:T(8,128)(2,1)}) custom-call(s32[1]{0:T(128)} %bitcast.me_ref, s32[32,8]{1,0:T(8,128)} %copy.22.up_idx, s32[32,8]{1,0:T(8,128)} %copy.23.down_idx, bf16[192,16384]{1,0:T(8,128)(2,1)} %all-gather.3.cloned.1.call-done.rows.mine_hbm, ...), custom_call_target="tpu_custom_call" | custom-call | bytes 44280000 | tf_op jit(solution)/shard_map/grad_chunk/pallas_call | solution.py:257
  162.5 1.5 collective-permute-start.13
  164.0 10.7 %grad_chunk.5 = (f32[8,2,128,128]{3,2,1,0:T(8,128)}, f32[8,2,128,128]{3,2,1,0:T(8,128)}, bf16[2,8,2,128,128]{4,3,2,1,0:T(8,128)(2,1)}) custom-call(s32[1]{0:T(128)} %bitcast.me_ref, s32[32,8]{1,0:T(8,128)} %copy.22.up_idx, s32[32,8]{1,0:T(8,128)} %copy.23.down_idx, bf16[192,16384]{1,0:T(8,128)(2,1)} %all-gather.3.cloned.1.call-done.rows.mine_hbm, ...), custom_call_target="tpu_custom_call" | custom-call | bytes 44280000 | tf_op jit(solution)/shard_map/grad_chunk/pallas_call | solution.py:257
  174.7 2.3 collective-permute-done.11.refs_4_.refs_3_
  178.3 23.7 %forward_last.1 = (bf16[2,16,192,128]{3,2,1,0:T(8,128)(2,1)}, bf16[192,16384]{1,0:T(8,128)(2,1)}) custom-call(s32[1]{0:T(128)} %bitcast.me_ref, s32[32,8]{1,0:T(8,128)} %copy.22.up_idx, s32[32,8]{1,0:T(8,128)} %copy.23.down_idx, bf16[192,16384]{1,0:T(8,128)(2,1)} %all-gather.3.cloned.1.call-done.rows.mine_hbm, f32[192,16384]{1,0:T(8,128)} %get-tuple-element.52.refs_0_, ...), custom_call_target="tpu_custom_call" | custom-call | bytes 73800000 | tf_op jit(solution)/shard_map/forward_last/pallas_call | solution.py:214
  202.7 10.9 %grad_chunk.6 = (f32[8,2,128,128]{3,2,1,0:T(8,128)}, f32[8,2,128,128]{3,2,1,0:T(8,128)}, bf16[2,8,2,128,128]{4,3,2,1,0:T(8,128)(2,1)}) custom-call(s32[1]{0:T(128)} %bitcast.me_ref, s32[32,8]{1,0:T(8,128)} %copy.22.up_idx, s32[32,8]{1,0:T(8,128)} %copy.23.down_idx, bf16[192,16384]{1,0:T(8,128)(2,1)} %all-gather.3.cloned.1.call-done.rows.mine_hbm, ...), custom_call_target="tpu_custom_call" | custom-call | bytes 44280000 | tf_op jit(solution)/shard_map/grad_chunk/pallas_call | solution.py:257
  213.6 1.6 collective-permute-start.15
  215.1 10.8 %grad_chunk.7 = (f32[8,2,128,128]{3,2,1,0:T(8,128)}, f32[8,2,128,128]{3,2,1,0:T(8,128)}, bf16[2,8,2,128,128]{4,3,2,1,0:T(8,128)(2,1)}) custom-call(s32[1]{0:T(128)} %bitcast.me_ref, s32[32,8]{1,0:T(8,128)} %copy.22.up_idx, s32[32,8]{1,0:T(8,128)} %copy.23.down_idx, bf16[192,16384]{1,0:T(8,128)(2,1)} %all-gather.3.cloned.1.call-done.rows.mine_hbm, ...), custom_call_target="tpu_custom_call" | custom-call | bytes 44280000 | tf_op jit(solution)/shard_map/grad_chunk/pallas_call | solution.py:257
  226.5 2.9 %finish_chunk.4 = (f32[32,2,128,128]{3,2,1,0:T(8,128)}, f32[32,2,128,128]{3,2,1,0:T(8,128)}) custom-call(f32[8,2,128,128]{3,2,1,0:T(8,128)} %get-tuple-element.72.own_up, f32[8,2,128,128]{3,2,1,0:T(8,128)} %get-tuple-element.73.own_down, bf16[2,8,2,128,128]{4,3,2,1,0:T(8,128)(2,1)} %copy-done.10), custom_call_target="tpu_custom_call" | custom-call | bytes 11070000 | tf_op jit(solution)/shard_map/finish_chunk/pallas_call | solution.py:284
  230.4 3.0 %finish_chunk.5 = (f32[32,2,128,128]{3,2,1,0:T(8,128)}, f32[32,2,128,128]{3,2,1,0:T(8,128)}) custom-call(f32[8,2,128,128]{3,2,1,0:T(8,128)} %get-tuple-element.69.own_up, f32[8,2,128,128]{3,2,1,0:T(8,128)} %get-tuple-element.70.own_down, bf16[2,8,2,128,128]{4,3,2,1,0:T(8,128)(2,1)} %copy-done.12, ...), custom_call_target="tpu_custom_call", output_to_operand_aliasing={{0}: (3, {}), {1}: (4, {})} | custom-call | bytes 11070000 | tf_op jit(solution)/shard_map/finish_chunk/pallas_call | solution.py:284
  233.4 17.5 %collective-permute-done.15.refs_0_ = bf16[2,8,2,128,128]{4,3,2,1,0:T(8,128)(2,1)S(1)} collective-permute-done((bf16[2,8,2,128,128]{4,3,2,1,0:T(8,128)(2,1)}, bf16[2,8,2,128,128]{4,3,2,1,0:T(8,128)(2,1)S(1)}, u32[]{:S(2)}, u32[]{:S(2)}) %collective-permute-start.15) | collective-permute-done | bytes 1048608 | tf_op jit(solution)/shard_map/ppermute | solution.py:302
  251.9 2.9 %finish_chunk.6 = (f32[32,2,128,128]{3,2,1,0:T(8,128)}, f32[32,2,128,128]{3,2,1,0:T(8,128)}) custom-call(f32[8,2,128,128]{3,2,1,0:T(8,128)} %get-tuple-element.66.own_up, f32[8,2,128,128]{3,2,1,0:T(8,128)} %get-tuple-element.67.own_down, bf16[2,8,2,128,128]{4,3,2,1,0:T(8,128)(2,1)} %copy-done.11, ...), custom_call_target="tpu_custom_call", output_to_operand_aliasing={{0}: (3, {}), {1}: (4, {})} | custom-call | bytes 11070000 | tf_op jit(solution)/shard_map/finish_chunk/pallas_call | solution.py:284
  254.9 10.7 %collective-permute-done.14.refs_0_ = bf16[2,8,2,128,128]{4,3,2,1,0:T(8,128)(2,1)S(1)} collective-permute-done((bf16[2,8,2,128,128]{4,3,2,1,0:T(8,128)(2,1)}, bf16[2,8,2,128,128]{4,3,2,1,0:T(8,128)(2,1)S(1)}, u32[]{:S(2)}, u32[]{:S(2)}) %collective-permute-start.14) | collective-permute-done | bytes 1048608 | tf_op jit(solution)/shard_map/ppermute | solution.py:302
  266.5 2.9 %finish_chunk.7 = (f32[32,2,128,128]{3,2,1,0:T(8,128)}, f32[32,2,128,128]{3,2,1,0:T(8,128)}) custom-call(f32[8,2,128,128]{3,2,1,0:T(8,128)} %get-tuple-element.63.own_up, f32[8,2,128,128]{3,2,1,0:T(8,128)} %get-tuple-element.64.own_down, bf16[2,8,2,128,128]{4,3,2,1,0:T(8,128)(2,1)} %copy-done.13, ...), custom_call_target="tpu_custom_call", output_to_operand_aliasing={{0}: (3, {}), {1}: (4, {})} | custom-call | bytes 11070000 | tf_op jit(solution)/shard_map/finish_chunk/pallas_call | solution.py:284
  269.5 2.0 reduce-scatter.2.cloned.1.call-done
  271.4 2.0 fusion.2
  (60 shorter events, 12.2 us)
Async XLA Ops:
  7.2 101.9 %all-gather.3.cloned.1.call-start = ((), (), s32[]{:S(2)}) async-start(), calls=%async_computation.1 | async-start | bytes 7077888 | tf_op jit(solution)/shard_map/all_gather | solution.py:327
  10.2 97.5 %copy-start.14 = (s32[32,8]{0,1:T(8,128)S(1)}, s32[32,8]{0,1:T(8,128)}, u32[]{:S(2)}) copy-start(s32[32,8]{0,1:T(8,128)} %param.10) | copy-start | bytes 3076
  10.2 98.2 %copy-start.15 = (s32[32,8]{0,1:T(8,128)S(1)}, s32[32,8]{0,1:T(8,128)}, u32[]{:S(2)}) copy-start(s32[32,8]{0,1:T(8,128)} %param.11) | copy-start | bytes 3076
  10.2 141.6 %all-gather.5.cloned.1.call-start = ((), (), s32[]{:S(2)}) async-start(), calls=%async_computation.2 | async-start | bytes 7077888 | tf_op jit(solution)/shard_map/all_gather | solution.py:336
  10.2 4.9 %copy-start.7 = (bf16[32,2,128,128]{3,2,1,0:T(8,128)(2,1)S(1)}, bf16[32,2,128,128]{3,2,1,0:T(8,128)(2,1)}, u32[]{:S(2)}) copy-start(bf16[32,2,128,128]{3,2,1,0:T(8,128)(2,1)} %param.9) | copy-start | bytes 6291460
  10.3 8.5 %copy-start.9 = (bf16[24,16384]{1,0:T(8,128)(2,1)S(1)}, bf16[24,16384]{1,0:T(8,128)(2,1)}, u32[]{:S(2)}) copy-start(bf16[24,16384]{1,0:T(8,128)(2,1)} %copy-done.8) | copy-start | bytes 2359300
  12.1 96.9 %copy-start.2 = (bf16[16,2,128,128]{3,2,1,0:T(8,128)(2,1)}, bf16[16,2,128,128]{3,2,1,0:T(8,128)(2,1)S(1)}, u32[]{:S(2)}) copy-start(bf16[16,2,128,128]{3,2,1,0:T(8,128)(2,1)S(1)} %get-tuple-element.85.refs_0_) | copy-start | bytes 3145732
  12.1 117.5 %copy-start = (bf16[16,2,128,128]{3,2,1,0:T(8,128)(2,1)}, bf16[16,2,128,128]{3,2,1,0:T(8,128)(2,1)S(1)}, u32[]{:S(2)}) copy-start(bf16[16,2,128,128]{3,2,1,0:T(8,128)(2,1)S(1)} %get-tuple-element.44.refs_1_.refs_0_) | copy-start | bytes 3145732
  12.1 65.6 %collective-permute-start.1 = (bf16[16,2,128,128]{3,2,1,0:T(8,128)(2,1)S(1)}, bf16[16,2,128,128]{3,2,1,0:T(8,128)(2,1)}, u32[]{:S(2)}, u32[]{:S(2)}) collective-permute-start(bf16[16,2,128,128]{3,2,1,0:T(8,128)(2,1)S(1)} %get-tuple-element.85.refs_0_), channel_id=1, source_target_pairs={{0,8},{8,0},{16,24},{24,16},{1,9},{9,1},{17,25},{25,17},{2,10},{10... | collective-permute-start | bytes 3145736 | tf_op jit(solution)/shard_map/ppermute | solution.py:302
  16.2 113.4 %copy-start.1 = (bf16[16,2,128,128]{3,2,1,0:T(8,128)(2,1)}, bf16[16,2,128,128]{3,2,1,0:T(8,128)(2,1)S(1)}, u32[]{:S(2)}) copy-start(bf16[16,2,128,128]{3,2,1,0:T(8,128)(2,1)S(1)} %get-tuple-element.45.refs_5_.refs_4_) | copy-start | bytes 3145732
  16.2 61.5 %collective-permute-start.2 = (bf16[16,2,128,128]{3,2,1,0:T(8,128)(2,1)}, bf16[16,2,128,128]{3,2,1,0:T(8,128)(2,1)}, u32[]{:S(2)}, u32[]{:S(2)}) collective-permute-start(bf16[16,2,128,128]{3,2,1,0:T(8,128)(2,1)} %get-tuple-element.83.refs_4_), channel_id=1, source_target_pairs={{0,16},{8,24},{16,0},{24,8},{1,17},{9,25},{17,1},{25,9},{2,18},{10... | collective-permute-start | bytes 3145736 | tf_op jit(solution)/shard_map/ppermute | solution.py:302
  17.8 60.0 %collective-permute-start.3 = (bf16[16,2,128,128]{3,2,1,0:T(8,128)(2,1)S(1)}, bf16[16,2,128,128]{3,2,1,0:T(8,128)(2,1)}, u32[]{:S(2)}, u32[]{:S(2)}) collective-permute-start(bf16[16,2,128,128]{3,2,1,0:T(8,128)(2,1)S(1)} %get-tuple-element.85.refs_0_), channel_id=1, source_target_pairs={{0,16},{8,24},{16,0},{24,8},{1,17},{9,25},{17,1},{25,9},{2,18},{10... | collective-permute-start | bytes 3145736 | tf_op jit(solution)/shard_map/ppermute | solution.py:302
  18.3 59.5 %collective-permute-start.4 = (bf16[16,2,128,128]{3,2,1,0:T(8,128)(2,1)}, bf16[16,2,128,128]{3,2,1,0:T(8,128)(2,1)}, u32[]{:S(2)}, u32[]{:S(2)}) collective-permute-start(bf16[16,2,128,128]{3,2,1,0:T(8,128)(2,1)} %get-tuple-element.83.refs_4_), channel_id=1, source_target_pairs={{0,8},{8,0},{16,24},{24,16},{1,9},{9,1},{17,25},{25,17},{2,10},{10... | collective-permute-start | bytes 3145736 | tf_op jit(solution)/shard_map/ppermute | solution.py:302
  18.7 59.0 %collective-permute-start = (bf16[24,16384]{1,0:T(8,128)(2,1)S(1)}, bf16[24,16384]{1,0:T(8,128)(2,1)}, u32[]{:S(2)}, u32[]{:S(2)}) collective-permute-start(bf16[24,16384]{1,0:T(8,128)(2,1)S(1)} %copy-done.9), channel_id=1, source_target_pairs={{0,8},{8,0},{16,24},{24,16},{1,9},{9,1},{17,25},{25,17},{2,10},{10... | collective-permute-start | bytes 2359304 | tf_op jit(solution)/shard_map/ppermute | solution.py:302
  77.8 193.7 %reduce-scatter.2.cloned.1.call-start = ((), (), s32[]{:S(2)}) async-start(), calls=%async_computation.3 | async-start | bytes 7077888 | tf_op jit(solution)/shard_map/reduce_scatter | solution.py:358
  77.8 24.6 %collective-permute-start.5 = (bf16[16,2,128,128]{3,2,1,0:T(8,128)(2,1)}, bf16[16,2,128,128]{3,2,1,0:T(8,128)(2,1)S(1)}, u32[]{:S(2)}, u32[]{:S(2)}) collective-permute-start(bf16[16,2,128,128]{3,2,1,0:T(8,128)(2,1)} %collective-permute-done.1.refs_1_), channel_id=1, source_target_pairs={{0,16},{8,24},{16,0},{24,8},{1,17},{9,25},{17,1},{25,9},{2,18},{10... | collective-permute-start | bytes 3145736 | tf_op jit(solution)/shard_map/ppermute | solution.py:302
  79.6 24.0 %collective-permute-start.6 = (bf16[16,2,128,128]{3,2,1,0:T(8,128)(2,1)}, bf16[16,2,128,128]{3,2,1,0:T(8,128)(2,1)S(1)}, u32[]{:S(2)}, u32[]{:S(2)}) collective-permute-start(bf16[16,2,128,128]{3,2,1,0:T(8,128)(2,1)} %collective-permute-done.2.refs_6_), channel_id=1, source_target_pairs={{0,8},{8,0},{16,24},{24,16},{1,9},{9,1},{17,25},{25,17},{2,10},{10... | collective-permute-start | bytes 3145736 | tf_op jit(solution)/shard_map/ppermute | solution.py:302
  102.4 3.2 %copy-start.3 = (bf16[16,2,128,128]{3,2,1,0:T(8,128)(2,1)}, bf16[16,2,128,128]{3,2,1,0:T(8,128)(2,1)S(1)}, u32[]{:S(2)}) copy-start(bf16[16,2,128,128]{3,2,1,0:T(8,128)(2,1)S(1)} %collective-permute-done.5.refs_3_) | copy-start | bytes 3145732
  103.6 3.5 %copy-start.4 = (bf16[16,2,128,128]{3,2,1,0:T(8,128)(2,1)}, bf16[16,2,128,128]{3,2,1,0:T(8,128)(2,1)S(1)}, u32[]{:S(2)}) copy-start(bf16[16,2,128,128]{3,2,1,0:T(8,128)(2,1)S(1)} %collective-permute-done.6.refs_7_) | copy-start | bytes 3145732
  103.6 26.2 %collective-permute-start.7 = (bf16[16,2,128,128]{3,2,1,0:T(8,128)(2,1)S(1)}, bf16[16,2,128,128]{3,2,1,0:T(8,128)(2,1)}, u32[]{:S(2)}, u32[]{:S(2)}) collective-permute-start(bf16[16,2,128,128]{3,2,1,0:T(8,128)(2,1)S(1)} %get-tuple-element.44.refs_1_.refs_0_), channel_id=1, source_target_pairs={{0,8},{8,0},{16,24},{24,16},{1,9},{9,1},{17,25},{25,17},{2,10},{10... | collective-permute-start | bytes 3145736 | tf_op jit(solution)/shard_map/ppermute | solution.py:302
  105.1 26.2 %collective-permute-start.8 = (bf16[16,2,128,128]{3,2,1,0:T(8,128)(2,1)S(1)}, bf16[16,2,128,128]{3,2,1,0:T(8,128)(2,1)}, u32[]{:S(2)}, u32[]{:S(2)}) collective-permute-start(bf16[16,2,128,128]{3,2,1,0:T(8,128)(2,1)S(1)} %get-tuple-element.45.refs_5_.refs_4_), channel_id=1, source_target_pairs={{0,16},{8,24},{16,0},{24,8},{1,17},{9,25},{17,1},{25,9},{2,18},{10... | collective-permute-start | bytes 3145736 | tf_op jit(solution)/shard_map/ppermute | solution.py:302
  105.6 45.1 %collective-permute-start.9 = (bf16[16,2,128,128]{3,2,1,0:T(8,128)(2,1)S(1)}, bf16[16,2,128,128]{3,2,1,0:T(8,128)(2,1)}, u32[]{:S(2)}, u32[]{:S(2)}) collective-permute-start(bf16[16,2,128,128]{3,2,1,0:T(8,128)(2,1)S(1)} %get-tuple-element.44.refs_1_.refs_0_), channel_id=1, source_target_pairs={{0,16},{8,24},{16,0},{24,8},{1,17},{9,25},{17,1},{25,9},{2,18},{10... | collective-permute-start | bytes 3145736 | tf_op jit(solution)/shard_map/ppermute | solution.py:302
  107.1 43.5 %collective-permute-start.10 = (bf16[16,2,128,128]{3,2,1,0:T(8,128)(2,1)S(1)}, bf16[16,2,128,128]{3,2,1,0:T(8,128)(2,1)}, u32[]{:S(2)}, u32[]{:S(2)}) collective-permute-start(bf16[16,2,128,128]{3,2,1,0:T(8,128)(2,1)S(1)} %get-tuple-element.45.refs_5_.refs_4_), channel_id=1, source_target_pairs={{0,8},{8,0},{16,24},{24,16},{1,9},{9,1},{17,25},{25,17},{2,10},{10... | collective-permute-start | bytes 3145736 | tf_op jit(solution)/shard_map/ppermute | solution.py:302
  150.7 26.3 %collective-permute-start.11 = (bf16[16,2,128,128]{3,2,1,0:T(8,128)(2,1)}, bf16[16,2,128,128]{3,2,1,0:T(8,128)(2,1)S(1)}, u32[]{:S(2)}, u32[]{:S(2)}) collective-permute-start(bf16[16,2,128,128]{3,2,1,0:T(8,128)(2,1)} %collective-permute-done.7.refs_2_.refs_1_), channel_id=1, source_target_pairs={{0,16},{8,24},{16,0},{24,8},{1,17},{9,25},{17,1},{25,9},{2,18},{10... | collective-permute-start | bytes 3145736 | tf_op jit(solution)/shard_map/ppermute | solution.py:302
  151.2 25.8 %collective-permute-start.12 = (bf16[16,2,128,128]{3,2,1,0:T(8,128)(2,1)}, bf16[16,2,128,128]{3,2,1,0:T(8,128)(2,1)S(1)}, u32[]{:S(2)}, u32[]{:S(2)}) collective-permute-start(bf16[16,2,128,128]{3,2,1,0:T(8,128)(2,1)} %collective-permute-done.8.refs_7_.refs_6_), channel_id=1, source_target_pairs={{0,8},{8,0},{16,24},{24,16},{1,9},{9,1},{17,25},{25,17},{2,10},{10... | collective-permute-start | bytes 3145736 | tf_op jit(solution)/shard_map/ppermute | solution.py:302
  162.5 39.6 %collective-permute-start.13 = (bf16[2,8,2,128,128]{4,3,2,1,0:T(8,128)(2,1)}, bf16[2,8,2,128,128]{4,3,2,1,0:T(8,128)(2,1)S(1)}, u32[]{:S(2)}, u32[]{:S(2)}) collective-permute-start(bf16[2,8,2,128,128]{4,3,2,1,0:T(8,128)(2,1)} %get-tuple-element.48), channel_id=1, source_target_pairs={{0,16},{8,24},{16,0},{24,8},{1,17},{9,25},{17,1},{25,9},{2,18},{10... | collective-permute-start | bytes 3145736 | tf_op jit(solution)/shard_map/ppermute | solution.py:302
  177.0 1.3 copy-start.6
  202.1 11.5 %copy-start.10 = (bf16[2,8,2,128,128]{4,3,2,1,0:T(8,128)(2,1)}, bf16[2,8,2,128,128]{4,3,2,1,0:T(8,128)(2,1)S(1)}, u32[]{:S(2)}) copy-start(bf16[2,8,2,128,128]{4,3,2,1,0:T(8,128)(2,1)S(1)} %collective-permute-done.13.refs_0_) | copy-start | bytes 3145732
  202.1 27.4 %collective-permute-start.16 = (bf16[2,8,2,128,128]{4,3,2,1,0:T(8,128)(2,1)}, bf16[2,8,2,128,128]{4,3,2,1,0:T(8,128)(2,1)S(1)}, u32[]{:S(2)}, u32[]{:S(2)}) collective-permute-start(bf16[2,8,2,128,128]{4,3,2,1,0:T(8,128)(2,1)} %get-tuple-element.50), channel_id=1, source_target_pairs={{0,16},{8,24},{16,0},{24,8},{1,17},{9,25},{17,1},{25,9},{2,18},{10... | collective-permute-start | bytes 3145736 | tf_op jit(solution)/shard_map/ppermute | solution.py:302
  213.6 37.4 %collective-permute-start.15 = (bf16[2,8,2,128,128]{4,3,2,1,0:T(8,128)(2,1)}, bf16[2,8,2,128,128]{4,3,2,1,0:T(8,128)(2,1)S(1)}, u32[]{:S(2)}, u32[]{:S(2)}) collective-permute-start(bf16[2,8,2,128,128]{4,3,2,1,0:T(8,128)(2,1)} %get-tuple-element.59), channel_id=1, source_target_pairs={{0,16},{8,24},{16,0},{24,8},{1,17},{9,25},{17,1},{25,9},{2,18},{10... | collective-permute-start | bytes 3145736 | tf_op jit(solution)/shard_map/ppermute | solution.py:302
  225.9 39.6 %collective-permute-start.14 = (bf16[2,8,2,128,128]{4,3,2,1,0:T(8,128)(2,1)}, bf16[2,8,2,128,128]{4,3,2,1,0:T(8,128)(2,1)S(1)}, u32[]{:S(2)}, u32[]{:S(2)}) collective-permute-start(bf16[2,8,2,128,128]{4,3,2,1,0:T(8,128)(2,1)} %get-tuple-element.62), channel_id=1, source_target_pairs={{0,16},{8,24},{16,0},{24,8},{1,17},{9,25},{17,1},{25,9},{2,18},{10... | collective-permute-start | bytes 3145736 | tf_op jit(solution)/shard_map/ppermute | solution.py:302
  250.9 1.0 copy-start.11
  (4 other events, 3.8 us)
Sparse Core Ops, SparseCore 0:
  10.3 67.4 all-gather.2
  79.4 64.7 all-gather.4
  202.2 69.1 reduce-scatter.1

commit v2 on v1

--- a/solution.py
+++ b/solution.py
@@ -58,20 +58,19 @@
             total[:, at] += terms[:, s * BLK : (s + 1) * BLK]
 
 
-def forward_kernel(n, firsts, resumed, me_ref, up_idx, down_idx, rows, *refs):
-    groups = len(firsts)
+def forward_kernel(n, first, half, resumed, me_ref, up_idx, down_idx, rows, *refs):
     if resumed:
         partial, refs = refs[0], refs[1:]
-    ups = [refs[2 * n * g : 2 * n * g + n] for g in range(groups)]
-    downs = [refs[2 * n * g + n : 2 * n * (g + 1)] for g in range(groups)]
-    hs, out_ref = refs[2 * n * groups : (2 * n + 1) * groups], refs[(2 * n + 1) * groups]
-    total = refs[-2] if resumed else out_ref
-    per_step = ups[0][0].shape[0]
+    ups, downs, (h_ref, out_ref) = refs[:n], refs[n : 2 * n], refs[2 * n : 2 * n + 2]
+    total, held = refs[-5:-3] if resumed else (out_ref, refs[-1])
+    per_step = ups[0].shape[0]
+    inner = min(4, per_step)
     width = rows.shape[1] // 2
     step = pl.program_id(0)
     me = me_ref[0]
     if resumed:
-        copy = pltpu.make_async_copy(partial, total, refs[-1])
+        rounded, sem, out_sems = refs[-3:]
+        copy = pltpu.make_async_copy(partial, total, sem)
 
     @pl.when(step == 0)
     def _():
@@ -84,32 +83,56 @@
                 at = pl.ds(pl.multiple_of(i * 16, 16), 16)
                 total[at] = jnp.zeros((16, total.shape[1]), total.dtype)
 
-    blocks = [(g, jj) for g in range(groups) for jj in range(per_step)]
-    for g, jj in blocks:
-        j = firsts[g] + step * per_step + jj
-        hidden, pre_grad = hidden_pair(n, j, jj, me, up_idx, down_idx, rows, ups[g], downs[g])
-        hs[g][0, jj] = hidden
-        hs[g][1, jj] = pre_grad
+    @pl.when(step < half)
+    def _():
+        @pl.loop(0, per_step // inner)
+        def _(i):
+            for jj in [i * inner + p for p in range(inner)]:
+                at = step * per_step + jj
+                hidden, pre_grad = hidden_pair(
+                    n, first + at, jj, me, up_idx, down_idx, rows, ups, downs
+                )
+                h_ref[0, jj] = hidden
+                h_ref[1, jj] = pre_grad
+                held[0, at] = hidden
+                held[1, at] = pre_grad
 
     if resumed:
 
-        @pl.when(step == 0)
+        @pl.when(step == half)
         def _():
             copy.wait()
 
-    for g, jj in blocks:
-        j = firsts[g] + step * per_step + jj
-        add_spread(n, j, jj, me, down_idx, hs[g][0, jj], downs[g], total, 0, 0)
-        add_spread(n, j, jj, me, up_idx, hs[g][1, jj], ups[g], total, width, 1)
+    @pl.when(step >= half)
+    def _():
+        @pl.loop(0, per_step // inner)
+        def _(i):
+            for jj in [i * inner + p for p in range(inner)]:
+                at = (step - half) * per_step + jj
+                j = first + at
+                add_spread(n, j, jj, me, down_idx, held[0, at], downs, total, 0, 0)
+                add_spread(n, j, jj, me, up_idx, held[1, at], ups, total, width, 1)
 
     if resumed:
 
         @pl.when(step == pl.num_programs(0) - 1)
         def _():
-            @pl.loop(0, total.shape[0] // 16)
-            def _(i):
-                at = pl.ds(pl.multiple_of(i * 16, 16), 16)
-                out_ref[at] = total[at].astype(out_ref.dtype)
+            part = total.shape[0] // 4
+            writes = []
+            for q in range(4):
+
+                @pl.loop(0, part // 16)
+                def _(i, q=q):
+                    at = pl.ds(pl.multiple_of(q * part + i * 16, 16), 16)
+                    rounded[at] = total[at].astype(rounded.dtype)
+
+                span = pl.ds(q * part, part)
+                writes.append(
+                    pltpu.make_async_copy(rounded.at[span], out_ref.at[span], out_sems.at[q])
+                )
+                writes[-1].start()
+            for write in writes:
+                write.wait()
 
 
 def grad_kernel(n, first, per_step, half, me_ref, up_idx, down_idx, mine_hbm, other_hbm, h_mine, *refs):
@@ -205,22 +228,32 @@
 def forward(n, first, per_group, me, up_index, down_index, rows, ups, downs, partial=None):
     resumed = partial is not None
     count = rows.shape[0]
-    per_step = min(4, per_group)
-    h_spec = pl.BlockSpec((2, per_step, count, BLK), lambda i: (0, i, 0, 0))
+    per_step = min(8, per_group)
+    half = per_group // per_step
+    h_spec = pl.BlockSpec((2, per_step, count, BLK), lambda i: (0, jnp.minimum(i, half - 1), 0, 0))
     h_shape = jax.ShapeDtypeStruct((2, per_group, count, BLK), jnp.bfloat16)
     total = jax.ShapeDtypeStruct(rows.shape, jnp.bfloat16 if resumed else jnp.float32)
-    scratch = [pltpu.VMEM(rows.shape, jnp.float32), pltpu.SemaphoreType.DMA]
+    held = pltpu.VMEM(h_shape.shape, h_shape.dtype)
+    scratch = [held]
+    if resumed:
+        scratch = [
+            pltpu.VMEM(rows.shape, jnp.float32),
+            held,
+            pltpu.VMEM(rows.shape, jnp.bfloat16),
+            pltpu.SemaphoreType.DMA,
+            pltpu.SemaphoreType.DMA((4,)),
+        ]
     pieces = ups + downs
     return pl.pallas_call(
-        functools.partial(forward_kernel, n, [first], resumed),
-        grid=(per_group // per_step,),
+        functools.partial(forward_kernel, n, first, half, resumed),
+        grid=(2 * half,),
         in_specs=[smem()] * 3
         + [whole(rows.shape)]
         + [pl.BlockSpec(memory_space=pl.ANY)] * resumed
-        + [tiles(piece, per_step, lambda i: i) for piece in pieces],
-        out_specs=[h_spec, whole(rows.shape)],
+        + [tiles(piece, per_step, lambda i: lax.rem(i, half)) for piece in pieces],
+        out_specs=[h_spec, pl.BlockSpec(memory_space=pl.ANY) if resumed else whole(rows.shape)],
         out_shape=[h_shape, total],
-        scratch_shapes=scratch * resumed,
+        scratch_shapes=scratch,
         compiler_params=params(),
         cost_estimate=pl.CostEstimate(flops=0, bytes_accessed=int(20 * US), transcendentals=0),
         name="forward_last" if resumed else "forward_first",

time: 280 us -> 279 us (level)
  transfers between devices with their start and end apart: 20 -> 20, of which waited for: 10 -> 8; matrix products, arithmetic and copies ran while one was open for 2% -> 2% of each run, Pallas kernels for 35% -> 36%
where the time goes in v2:
time: 279 us; the launch traced here: 278 us
  waiting for transfers between devices  132 us (47%)
  Pallas kernels  99.4 us (36%)
  starting transfers between devices  19.9 us (7%)
  between operations  14 us (5%)
  local copies, waits for them, and re-layouts  13.5 us (5%)
    ppermute x17, waiting for transfers between devices, exchange(): return lax.ppermute(a, 'fsdp', [(i, i ^ bit) for i in range(n)])  130 us
    pallas_call x2, Pallas kernels, forward(): pl.pallas_call(functools.partial(forward_kernel, n, first, half, resumed)...  44.7 us
    pallas_call x4, Pallas kernels, grads(): pl.pallas_call(functools.partial(grad_kernel, n, start + at, per_step, ha...  43 us
    ppermute x17, starting transfers between devices, exchange(): return lax.ppermute(a, 'fsdp', [(i, i ^ bit) for i in range(n)])  19.8 us
    pallas_call x4, Pallas kernels, finish(): pl.pallas_call(functools.partial(finish_kernel, len(got)), grid=(per_chun...  11.8 us
    unnamed x35, local copies, waits for them, and re-layouts  7.55 us
  transfers between devices with their start and end apart: 20, of which 8 were waited for; matrix products, arithmetic and copies ran while one was open for 2% of the time, Pallas kernels for 36%

profile of v2, /device:TPU:0, one launch (start us, length us, event | category | flops | bytes accessed | tf_op | source)
XLA Modules:
  0.0 278.4 jit_solution(14463167975117308779)
XLA Ops:
  7.2 1.0 constant_dynamic-update-slice_fusion.1
  8.2 1.0 constant_dynamic-update-slice_fusion
  10.3 1.8 fusion.1
  12.1 3.0 %collective-permute-start.1 = (bf16[16,2,128,128]{3,2,1,0:T(8,128)(2,1)S(1)}, bf16[16,2,128,128]{3,2,1,0:T(8,128)(2,1)}, u32[]{:S(2)}, u32[]{:S(2)}) collective-permute-start(bf16[16,2,128,128]{3,2,1,0:T(8,128)(2,1)S(1)} %get-tuple-element.85.refs_0_), channel_id=1, source_target_pairs={{0,8},{8,0},{16,24},{24,16},{1,9},{9,1},{17,25},{25,17},{2,10},{10... | collective-permute-start | bytes 3145736 | tf_op jit(solution)/shard_map/ppermute | solution.py:335
  15.1 1.1 fusion
  16.2 1.5 collective-permute-start.2
  18.7 1.6 collective-permute-start
  20.3 57.4 %collective-permute-done = bf16[24,16384]{1,0:T(8,128)(2,1)} collective-permute-done((bf16[24,16384]{1,0:T(8,128)(2,1)S(1)}, bf16[24,16384]{1,0:T(8,128)(2,1)}, u32[]{:S(2)}, u32[]{:S(2)}) %collective-permute-start) | collective-permute-done | bytes 786464 | tf_op jit(solution)/shard_map/ppermute | solution.py:335
  77.8 1.8 collective-permute-start.5
  79.6 1.5 collective-permute-start.6
  81.1 21.3 %collective-permute-done.5.refs_3_ = bf16[16,2,128,128]{3,2,1,0:T(8,128)(2,1)S(1)} collective-permute-done((bf16[16,2,128,128]{3,2,1,0:T(8,128)(2,1)}, bf16[16,2,128,128]{3,2,1,0:T(8,128)(2,1)S(1)}, u32[]{:S(2)}, u32[]{:S(2)}) %collective-permute-start.5) | collective-permute-done | bytes 1048608 | tf_op jit(solution)/shard_map/ppermute | solution.py:335
  102.4 1.2 collective-permute-done.6.refs_7_
  103.6 1.5 collective-permute-start.7
  105.6 1.5 collective-permute-start.9
  109.0 22.6 %forward_first.1 = (bf16[2,16,192,128]{3,2,1,0:T(8,128)(2,1)}, f32[192,16384]{1,0:T(8,128)}) custom-call(s32[1]{0:T(128)} %bitcast.me_ref, s32[32,8]{1,0:T(8,128)} %copy.22.up_idx, s32[32,8]{1,0:T(8,128)} %copy.23.down_idx, bf16[192,16384]{1,0:T(8,128)(2,1)} %all-gather.3.cloned.1.call-done.rows.mine_hbm, bf16[16,2,128,128]{3,2,1,0:T(8,128)(2,1)} %copy-done.2, ...), custom_call_target="tpu_custom_call" | custom-call | bytes 73800000 | tf_op jit(solution)/shard_map/forward_first/pallas_call | solution.py:247
  131.7 19.0 %collective-permute-done.9.refs_3_.refs_2_ = bf16[16,2,128,128]{3,2,1,0:T(8,128)(2,1)} collective-permute-done((bf16[16,2,128,128]{3,2,1,0:T(8,128)(2,1)S(1)}, bf16[16,2,128,128]{3,2,1,0:T(8,128)(2,1)}, u32[]{:S(2)}, u32[]{:S(2)}) %collective-permute-start.9) | collective-permute-done | bytes 1048608 | tf_op jit(solution)/shard_map/ppermute | solution.py:335
  151.8 10.6 %grad_chunk.4 = (f32[8,2,128,128]{3,2,1,0:T(8,128)}, f32[8,2,128,128]{3,2,1,0:T(8,128)}, bf16[2,8,2,128,128]{4,3,2,1,0:T(8,128)(2,1)}) custom-call(s32[1]{0:T(128)} %bitcast.me_ref, s32[32,8]{1,0:T(8,128)} %copy.22.up_idx, s32[32,8]{1,0:T(8,128)} %copy.23.down_idx, bf16[192,16384]{1,0:T(8,128)(2,1)} %all-gather.3.cloned.1.call-done.rows.mine_hbm, ...), custom_call_target="tpu_custom_call" | custom-call | bytes 44280000 | tf_op jit(solution)/shard_map/grad_chunk/pallas_call | solution.py:290
  162.5 1.5 collective-permute-start.13
  164.0 10.7 %grad_chunk.5 = (f32[8,2,128,128]{3,2,1,0:T(8,128)}, f32[8,2,128,128]{3,2,1,0:T(8,128)}, bf16[2,8,2,128,128]{4,3,2,1,0:T(8,128)(2,1)}) custom-call(s32[1]{0:T(128)} %bitcast.me_ref, s32[32,8]{1,0:T(8,128)} %copy.22.up_idx, s32[32,8]{1,0:T(8,128)} %copy.23.down_idx, bf16[192,16384]{1,0:T(8,128)(2,1)} %all-gather.3.cloned.1.call-done.rows.mine_hbm, ...), custom_call_target="tpu_custom_call" | custom-call | bytes 44280000 | tf_op jit(solution)/shard_map/grad_chunk/pallas_call | solution.py:290
  174.7 2.3 collective-permute-done.11.refs_4_.refs_3_
  178.3 22.0 %forward_last.1 = (bf16[2,16,192,128]{3,2,1,0:T(8,128)(2,1)}, bf16[192,16384]{1,0:T(8,128)(2,1)}) custom-call(s32[1]{0:T(128)} %bitcast.me_ref, s32[32,8]{1,0:T(8,128)} %copy.22.up_idx, s32[32,8]{1,0:T(8,128)} %copy.23.down_idx, bf16[192,16384]{1,0:T(8,128)(2,1)} %all-gather.3.cloned.1.call-done.rows.mine_hbm, f32[192,16384]{1,0:T(8,128)} %get-tuple-element.52.refs_0_, ...), custom_call_target="tpu_custom_call" | custom-call | bytes 73800000 | tf_op jit(solution)/shard_map/forward_last/pallas_call | solution.py:247
  201.0 10.9 %grad_chunk.6 = (f32[8,2,128,128]{3,2,1,0:T(8,128)}, f32[8,2,128,128]{3,2,1,0:T(8,128)}, bf16[2,8,2,128,128]{4,3,2,1,0:T(8,128)(2,1)}) custom-call(s32[1]{0:T(128)} %bitcast.me_ref, s32[32,8]{1,0:T(8,128)} %copy.22.up_idx, s32[32,8]{1,0:T(8,128)} %copy.23.down_idx, bf16[192,16384]{1,0:T(8,128)(2,1)} %all-gather.3.cloned.1.call-done.rows.mine_hbm, ...), custom_call_target="tpu_custom_call" | custom-call | bytes 44280000 | tf_op jit(solution)/shard_map/grad_chunk/pallas_call | solution.py:290
  211.9 1.6 collective-permute-start.15
  213.5 10.7 %grad_chunk.7 = (f32[8,2,128,128]{3,2,1,0:T(8,128)}, f32[8,2,128,128]{3,2,1,0:T(8,128)}, bf16[2,8,2,128,128]{4,3,2,1,0:T(8,128)(2,1)}) custom-call(s32[1]{0:T(128)} %bitcast.me_ref, s32[32,8]{1,0:T(8,128)} %copy.22.up_idx, s32[32,8]{1,0:T(8,128)} %copy.23.down_idx, bf16[192,16384]{1,0:T(8,128)(2,1)} %all-gather.3.cloned.1.call-done.rows.mine_hbm, ...), custom_call_target="tpu_custom_call" | custom-call | bytes 44280000 | tf_op jit(solution)/shard_map/grad_chunk/pallas_call | solution.py:290
  224.8 2.9 %finish_chunk.4 = (f32[32,2,128,128]{3,2,1,0:T(8,128)}, f32[32,2,128,128]{3,2,1,0:T(8,128)}) custom-call(f32[8,2,128,128]{3,2,1,0:T(8,128)} %get-tuple-element.72.own_up, f32[8,2,128,128]{3,2,1,0:T(8,128)} %get-tuple-element.73.own_down, bf16[2,8,2,128,128]{4,3,2,1,0:T(8,128)(2,1)} %copy-done.10), custom_call_target="tpu_custom_call" | custom-call | bytes 11070000 | tf_op jit(solution)/shard_map/finish_chunk/pallas_call | solution.py:317
  228.8 3.0 %finish_chunk.5 = (f32[32,2,128,128]{3,2,1,0:T(8,128)}, f32[32,2,128,128]{3,2,1,0:T(8,128)}) custom-call(f32[8,2,128,128]{3,2,1,0:T(8,128)} %get-tuple-element.69.own_up, f32[8,2,128,128]{3,2,1,0:T(8,128)} %get-tuple-element.70.own_down, bf16[2,8,2,128,128]{4,3,2,1,0:T(8,128)(2,1)} %copy-done.12, ...), custom_call_target="tpu_custom_call", output_to_operand_aliasing={{0}: (3, {}), {1}: (4, {})} | custom-call | bytes 11070000 | tf_op jit(solution)/shard_map/finish_chunk/pallas_call | solution.py:317
  231.7 17.5 %collective-permute-done.15.refs_0_ = bf16[2,8,2,128,128]{4,3,2,1,0:T(8,128)(2,1)S(1)} collective-permute-done((bf16[2,8,2,128,128]{4,3,2,1,0:T(8,128)(2,1)}, bf16[2,8,2,128,128]{4,3,2,1,0:T(8,128)(2,1)S(1)}, u32[]{:S(2)}, u32[]{:S(2)}) %collective-permute-start.15) | collective-permute-done | bytes 1048608 | tf_op jit(solution)/shard_map/ppermute | solution.py:335
  250.2 2.9 %finish_chunk.6 = (f32[32,2,128,128]{3,2,1,0:T(8,128)}, f32[32,2,128,128]{3,2,1,0:T(8,128)}) custom-call(f32[8,2,128,128]{3,2,1,0:T(8,128)} %get-tuple-element.66.own_up, f32[8,2,128,128]{3,2,1,0:T(8,128)} %get-tuple-element.67.own_down, bf16[2,8,2,128,128]{4,3,2,1,0:T(8,128)(2,1)} %copy-done.11, ...), custom_call_target="tpu_custom_call", output_to_operand_aliasing={{0}: (3, {}), {1}: (4, {})} | custom-call | bytes 11070000 | tf_op jit(solution)/shard_map/finish_chunk/pallas_call | solution.py:317
  253.2 10.8 %collective-permute-done.14.refs_0_ = bf16[2,8,2,128,128]{4,3,2,1,0:T(8,128)(2,1)S(1)} collective-permute-done((bf16[2,8,2,128,128]{4,3,2,1,0:T(8,128)(2,1)}, bf16[2,8,2,128,128]{4,3,2,1,0:T(8,128)(2,1)S(1)}, u32[]{:S(2)}, u32[]{:S(2)}) %collective-permute-start.14) | collective-permute-done | bytes 1048608 | tf_op jit(solution)/shard_map/ppermute | solution.py:335
  264.9 2.9 %finish_chunk.7 = (f32[32,2,128,128]{3,2,1,0:T(8,128)}, f32[32,2,128,128]{3,2,1,0:T(8,128)}) custom-call(f32[8,2,128,128]{3,2,1,0:T(8,128)} %get-tuple-element.63.own_up, f32[8,2,128,128]{3,2,1,0:T(8,128)} %get-tuple-element.64.own_down, bf16[2,8,2,128,128]{4,3,2,1,0:T(8,128)(2,1)} %copy-done.13, ...), custom_call_target="tpu_custom_call", output_to_operand_aliasing={{0}: (3, {}), {1}: (4, {})} | custom-call | bytes 11070000 | tf_op jit(solution)/shard_map/finish_chunk/pallas_call | solution.py:317
  267.9 1.9 reduce-scatter.2.cloned.1.call-done
  269.8 2.0 fusion.2
  (60 shorter events, 11.1 us)
Async XLA Ops:
  7.2 101.9 %all-gather.3.cloned.1.call-start = ((), (), s32[]{:S(2)}) async-start(), calls=%async_computation.1 | async-start | bytes 7077888 | tf_op jit(solution)/shard_map/all_gather | solution.py:360
  10.2 97.5 %copy-start.14 = (s32[32,8]{0,1:T(8,128)S(1)}, s32[32,8]{0,1:T(8,128)}, u32[]{:S(2)}) copy-start(s32[32,8]{0,1:T(8,128)} %param.10) | copy-start | bytes 3076
  10.2 98.2 %copy-start.15 = (s32[32,8]{0,1:T(8,128)S(1)}, s32[32,8]{0,1:T(8,128)}, u32[]{:S(2)}) copy-start(s32[32,8]{0,1:T(8,128)} %param.11) | copy-start | bytes 3076
  10.2 141.6 %all-gather.5.cloned.1.call-start = ((), (), s32[]{:S(2)}) async-start(), calls=%async_computation.2 | async-start | bytes 7077888 | tf_op jit(solution)/shard_map/all_gather | solution.py:369
  10.2 4.9 %copy-start.7 = (bf16[32,2,128,128]{3,2,1,0:T(8,128)(2,1)S(1)}, bf16[32,2,128,128]{3,2,1,0:T(8,128)(2,1)}, u32[]{:S(2)}) copy-start(bf16[32,2,128,128]{3,2,1,0:T(8,128)(2,1)} %param.9) | copy-start | bytes 6291460
  10.3 8.5 %copy-start.9 = (bf16[24,16384]{1,0:T(8,128)(2,1)S(1)}, bf16[24,16384]{1,0:T(8,128)(2,1)}, u32[]{:S(2)}) copy-start(bf16[24,16384]{1,0:T(8,128)(2,1)} %copy-done.8) | copy-start | bytes 2359300
  12.1 96.9 %copy-start.2 = (bf16[16,2,128,128]{3,2,1,0:T(8,128)(2,1)}, bf16[16,2,128,128]{3,2,1,0:T(8,128)(2,1)S(1)}, u32[]{:S(2)}) copy-start(bf16[16,2,128,128]{3,2,1,0:T(8,128)(2,1)S(1)} %get-tuple-element.85.refs_0_) | copy-start | bytes 3145732
  12.1 119.5 %copy-start = (bf16[16,2,128,128]{3,2,1,0:T(8,128)(2,1)}, bf16[16,2,128,128]{3,2,1,0:T(8,128)(2,1)S(1)}, u32[]{:S(2)}) copy-start(bf16[16,2,128,128]{3,2,1,0:T(8,128)(2,1)S(1)} %get-tuple-element.44.refs_1_.refs_0_) | copy-start | bytes 3145732
  12.1 65.6 %collective-permute-start.1 = (bf16[16,2,128,128]{3,2,1,0:T(8,128)(2,1)S(1)}, bf16[16,2,128,128]{3,2,1,0:T(8,128)(2,1)}, u32[]{:S(2)}, u32[]{:S(2)}) collective-permute-start(bf16[16,2,128,128]{3,2,1,0:T(8,128)(2,1)S(1)} %get-tuple-element.85.refs_0_), channel_id=1, source_target_pairs={{0,8},{8,0},{16,24},{24,16},{1,9},{9,1},{17,25},{25,17},{2,10},{10... | collective-permute-start | bytes 3145736 | tf_op jit(solution)/shard_map/ppermute | solution.py:335
  16.2 115.4 %copy-start.1 = (bf16[16,2,128,128]{3,2,1,0:T(8,128)(2,1)}, bf16[16,2,128,128]{3,2,1,0:T(8,128)(2,1)S(1)}, u32[]{:S(2)}) copy-start(bf16[16,2,128,128]{3,2,1,0:T(8,128)(2,1)S(1)} %get-tuple-element.45.refs_5_.refs_4_) | copy-start | bytes 3145732
  16.2 61.5 %collective-permute-start.2 = (bf16[16,2,128,128]{3,2,1,0:T(8,128)(2,1)}, bf16[16,2,128,128]{3,2,1,0:T(8,128)(2,1)}, u32[]{:S(2)}, u32[]{:S(2)}) collective-permute-start(bf16[16,2,128,128]{3,2,1,0:T(8,128)(2,1)} %get-tuple-element.83.refs_4_), channel_id=1, source_target_pairs={{0,16},{8,24},{16,0},{24,8},{1,17},{9,25},{17,1},{25,9},{2,18},{10... | collective-permute-start | bytes 3145736 | tf_op jit(solution)/shard_map/ppermute | solution.py:335
  17.8 60.0 %collective-permute-start.3 = (bf16[16,2,128,128]{3,2,1,0:T(8,128)(2,1)S(1)}, bf16[16,2,128,128]{3,2,1,0:T(8,128)(2,1)}, u32[]{:S(2)}, u32[]{:S(2)}) collective-permute-start(bf16[16,2,128,128]{3,2,1,0:T(8,128)(2,1)S(1)} %get-tuple-element.85.refs_0_), channel_id=1, source_target_pairs={{0,16},{8,24},{16,0},{24,8},{1,17},{9,25},{17,1},{25,9},{2,18},{10... | collective-permute-start | bytes 3145736 | tf_op jit(solution)/shard_map/ppermute | solution.py:335
  18.3 59.5 %collective-permute-start.4 = (bf16[16,2,128,128]{3,2,1,0:T(8,128)(2,1)}, bf16[16,2,128,128]{3,2,1,0:T(8,128)(2,1)}, u32[]{:S(2)}, u32[]{:S(2)}) collective-permute-start(bf16[16,2,128,128]{3,2,1,0:T(8,128)(2,1)} %get-tuple-element.83.refs_4_), channel_id=1, source_target_pairs={{0,8},{8,0},{16,24},{24,16},{1,9},{9,1},{17,25},{25,17},{2,10},{10... | collective-permute-start | bytes 3145736 | tf_op jit(solution)/shard_map/ppermute | solution.py:335
  18.7 59.0 %collective-permute-start = (bf16[24,16384]{1,0:T(8,128)(2,1)S(1)}, bf16[24,16384]{1,0:T(8,128)(2,1)}, u32[]{:S(2)}, u32[]{:S(2)}) collective-permute-start(bf16[24,16384]{1,0:T(8,128)(2,1)S(1)} %copy-done.9), channel_id=1, source_target_pairs={{0,8},{8,0},{16,24},{24,16},{1,9},{9,1},{17,25},{25,17},{2,10},{10... | collective-permute-start | bytes 2359304 | tf_op jit(solution)/shard_map/ppermute | solution.py:335
  77.8 192.0 %reduce-scatter.2.cloned.1.call-start = ((), (), s32[]{:S(2)}) async-start(), calls=%async_computation.3 | async-start | bytes 7077888 | tf_op jit(solution)/shard_map/reduce_scatter | solution.py:391
  77.8 24.6 %collective-permute-start.5 = (bf16[16,2,128,128]{3,2,1,0:T(8,128)(2,1)}, bf16[16,2,128,128]{3,2,1,0:T(8,128)(2,1)S(1)}, u32[]{:S(2)}, u32[]{:S(2)}) collective-permute-start(bf16[16,2,128,128]{3,2,1,0:T(8,128)(2,1)} %collective-permute-done.1.refs_1_), channel_id=1, source_target_pairs={{0,16},{8,24},{16,0},{24,8},{1,17},{9,25},{17,1},{25,9},{2,18},{10... | collective-permute-start | bytes 3145736 | tf_op jit(solution)/shard_map/ppermute | solution.py:335
  79.6 24.0 %collective-permute-start.6 = (bf16[16,2,128,128]{3,2,1,0:T(8,128)(2,1)}, bf16[16,2,128,128]{3,2,1,0:T(8,128)(2,1)S(1)}, u32[]{:S(2)}, u32[]{:S(2)}) collective-permute-start(bf16[16,2,128,128]{3,2,1,0:T(8,128)(2,1)} %collective-permute-done.2.refs_6_), channel_id=1, source_target_pairs={{0,8},{8,0},{16,24},{24,16},{1,9},{9,1},{17,25},{25,17},{2,10},{10... | collective-permute-start | bytes 3145736 | tf_op jit(solution)/shard_map/ppermute | solution.py:335
  102.4 3.2 %copy-start.3 = (bf16[16,2,128,128]{3,2,1,0:T(8,128)(2,1)}, bf16[16,2,128,128]{3,2,1,0:T(8,128)(2,1)S(1)}, u32[]{:S(2)}) copy-start(bf16[16,2,128,128]{3,2,1,0:T(8,128)(2,1)S(1)} %collective-permute-done.5.refs_3_) | copy-start | bytes 3145732
  103.6 3.5 %copy-start.4 = (bf16[16,2,128,128]{3,2,1,0:T(8,128)(2,1)}, bf16[16,2,128,128]{3,2,1,0:T(8,128)(2,1)S(1)}, u32[]{:S(2)}) copy-start(bf16[16,2,128,128]{3,2,1,0:T(8,128)(2,1)S(1)} %collective-permute-done.6.refs_7_) | copy-start | bytes 3145732
  103.6 28.1 %collective-permute-start.7 = (bf16[16,2,128,128]{3,2,1,0:T(8,128)(2,1)S(1)}, bf16[16,2,128,128]{3,2,1,0:T(8,128)(2,1)}, u32[]{:S(2)}, u32[]{:S(2)}) collective-permute-start(bf16[16,2,128,128]{3,2,1,0:T(8,128)(2,1)S(1)} %get-tuple-element.44.refs_1_.refs_0_), channel_id=1, source_target_pairs={{0,8},{8,0},{16,24},{24,16},{1,9},{9,1},{17,25},{25,17},{2,10},{10... | collective-permute-start | bytes 3145736 | tf_op jit(solution)/shard_map/ppermute | solution.py:335
  105.1 26.6 %collective-permute-start.8 = (bf16[16,2,128,128]{3,2,1,0:T(8,128)(2,1)S(1)}, bf16[16,2,128,128]{3,2,1,0:T(8,128)(2,1)}, u32[]{:S(2)}, u32[]{:S(2)}) collective-permute-start(bf16[16,2,128,128]{3,2,1,0:T(8,128)(2,1)S(1)} %get-tuple-element.45.refs_5_.refs_4_), channel_id=1, source_target_pairs={{0,16},{8,24},{16,0},{24,8},{1,17},{9,25},{17,1},{25,9},{2,18},{10... | collective-permute-start | bytes 3145736 | tf_op jit(solution)/shard_map/ppermute | solution.py:335
  105.6 45.1 %collective-permute-start.9 = (bf16[16,2,128,128]{3,2,1,0:T(8,128)(2,1)S(1)}, bf16[16,2,128,128]{3,2,1,0:T(8,128)(2,1)}, u32[]{:S(2)}, u32[]{:S(2)}) collective-permute-start(bf16[16,2,128,128]{3,2,1,0:T(8,128)(2,1)S(1)} %get-tuple-element.44.refs_1_.refs_0_), channel_id=1, source_target_pairs={{0,16},{8,24},{16,0},{24,8},{1,17},{9,25},{17,1},{25,9},{2,18},{10... | collective-permute-start | bytes 3145736 | tf_op jit(solution)/shard_map/ppermute | solution.py:335
  107.1 43.5 %collective-permute-start.10 = (bf16[16,2,128,128]{3,2,1,0:T(8,128)(2,1)S(1)}, bf16[16,2,128,128]{3,2,1,0:T(8,128)(2,1)}, u32[]{:S(2)}, u32[]{:S(2)}) collective-permute-start(bf16[16,2,128,128]{3,2,1,0:T(8,128)(2,1)S(1)} %get-tuple-element.45.refs_5_.refs_4_), channel_id=1, source_target_pairs={{0,8},{8,0},{16,24},{24,16},{1,9},{9,1},{17,25},{25,17},{2,10},{10... | collective-permute-start | bytes 3145736 | tf_op jit(solution)/shard_map/ppermute | solution.py:335
  150.7 26.3 %collective-permute-start.11 = (bf16[16,2,128,128]{3,2,1,0:T(8,128)(2,1)}, bf16[16,2,128,128]{3,2,1,0:T(8,128)(2,1)S(1)}, u32[]{:S(2)}, u32[]{:S(2)}) collective-permute-start(bf16[16,2,128,128]{3,2,1,0:T(8,128)(2,1)} %collective-permute-done.7.refs_2_.refs_1_), channel_id=1, source_target_pairs={{0,16},{8,24},{16,0},{24,8},{1,17},{9,25},{17,1},{25,9},{2,18},{10... | collective-permute-start | bytes 3145736 | tf_op jit(solution)/shard_map/ppermute | solution.py:335
  151.2 25.8 %collective-permute-start.12 = (bf16[16,2,128,128]{3,2,1,0:T(8,128)(2,1)}, bf16[16,2,128,128]{3,2,1,0:T(8,128)(2,1)S(1)}, u32[]{:S(2)}, u32[]{:S(2)}) collective-permute-start(bf16[16,2,128,128]{3,2,1,0:T(8,128)(2,1)} %collective-permute-done.8.refs_7_.refs_6_), channel_id=1, source_target_pairs={{0,8},{8,0},{16,24},{24,16},{1,9},{9,1},{17,25},{25,17},{2,10},{10... | collective-permute-start | bytes 3145736 | tf_op jit(solution)/shard_map/ppermute | solution.py:335
  162.5 37.9 %collective-permute-start.13 = (bf16[2,8,2,128,128]{4,3,2,1,0:T(8,128)(2,1)}, bf16[2,8,2,128,128]{4,3,2,1,0:T(8,128)(2,1)S(1)}, u32[]{:S(2)}, u32[]{:S(2)}) collective-permute-start(bf16[2,8,2,128,128]{4,3,2,1,0:T(8,128)(2,1)} %get-tuple-element.48), channel_id=1, source_target_pairs={{0,16},{8,24},{16,0},{24,8},{1,17},{9,25},{17,1},{25,9},{2,18},{10... | collective-permute-start | bytes 3145736 | tf_op jit(solution)/shard_map/ppermute | solution.py:335
  177.0 1.3 copy-start.6
  200.4 11.5 %copy-start.10 = (bf16[2,8,2,128,128]{4,3,2,1,0:T(8,128)(2,1)}, bf16[2,8,2,128,128]{4,3,2,1,0:T(8,128)(2,1)S(1)}, u32[]{:S(2)}) copy-start(bf16[2,8,2,128,128]{4,3,2,1,0:T(8,128)(2,1)S(1)} %collective-permute-done.13.refs_0_) | copy-start | bytes 3145732
  200.4 27.4 %collective-permute-start.16 = (bf16[2,8,2,128,128]{4,3,2,1,0:T(8,128)(2,1)}, bf16[2,8,2,128,128]{4,3,2,1,0:T(8,128)(2,1)S(1)}, u32[]{:S(2)}, u32[]{:S(2)}) collective-permute-start(bf16[2,8,2,128,128]{4,3,2,1,0:T(8,128)(2,1)} %get-tuple-element.50), channel_id=1, source_target_pairs={{0,16},{8,24},{16,0},{24,8},{1,17},{9,25},{17,1},{25,9},{2,18},{10... | collective-permute-start | bytes 3145736 | tf_op jit(solution)/shard_map/ppermute | solution.py:335
  211.9 37.4 %collective-permute-start.15 = (bf16[2,8,2,128,128]{4,3,2,1,0:T(8,128)(2,1)}, bf16[2,8,2,128,128]{4,3,2,1,0:T(8,128)(2,1)S(1)}, u32[]{:S(2)}, u32[]{:S(2)}) collective-permute-start(bf16[2,8,2,128,128]{4,3,2,1,0:T(8,128)(2,1)} %get-tuple-element.59), channel_id=1, source_target_pairs={{0,16},{8,24},{16,0},{24,8},{1,17},{9,25},{17,1},{25,9},{2,18},{10... | collective-permute-start | bytes 3145736 | tf_op jit(solution)/shard_map/ppermute | solution.py:335
  224.2 39.7 %collective-permute-start.14 = (bf16[2,8,2,128,128]{4,3,2,1,0:T(8,128)(2,1)}, bf16[2,8,2,128,128]{4,3,2,1,0:T(8,128)(2,1)S(1)}, u32[]{:S(2)}, u32[]{:S(2)}) collective-permute-start(bf16[2,8,2,128,128]{4,3,2,1,0:T(8,128)(2,1)} %get-tuple-element.62), channel_id=1, source_target_pairs={{0,16},{8,24},{16,0},{24,8},{1,17},{9,25},{17,1},{25,9},{2,18},{10... | collective-permute-start | bytes 3145736 | tf_op jit(solution)/shard_map/ppermute | solution.py:335
  249.3 1.0 copy-start.11
  (4 other events, 3.8 us)
Sparse Core Ops, SparseCore 0:
  10.3 67.4 all-gather.2
  79.4 64.7 all-gather.4
  200.5 69.2 reduce-scatter.1

commit v3 on v2

--- a/solution.py
+++ b/solution.py
@@ -335,11 +335,12 @@
     return lax.ppermute(a, "fsdp", [(i, i ^ bit) for i in range(n)])
 
 
-def gather(n, up, down, late=()):
+def gather(n, up, down, ends=(), late=()):
     bits = [1 << b for b in range(n.bit_length() - 1)]
     first, last = bits[0], bits[-1]
-    ups = {0: up, first: exchange(up, first, n), last: exchange(up, last, n)}
-    downs = {0: down, first: exchange(down, first, n), last: exchange(down, last, n)}
+    then_up, then_down = (after(up, *ends), after(down, *ends)) if ends else (up, down)
+    ups = {0: up, first: exchange(up, first, n), last: exchange(then_up, last, n)}
+    downs = {0: down, first: exchange(then_down, first, n), last: exchange(down, last, n)}
     marks = [ups[first], downs[last], ups[last], downs[first]]
     for held, order in ((ups, bits[1:]), (downs, bits[-2::-1])):
         for bit in order:
@@ -371,8 +372,8 @@
     h, partial = forward_group(0, mine)
     hs = [h]
     ends = (up[-1][0], down[-1][0])
-    up, down = after(up_weight[per_group:], *ends), after(down_weight[per_group:], *ends)
-    up, down, marks = gather(n, up, down, (h,))
+    up, down = after(up_weight[per_group:], *marks), after(down_weight[per_group:], *marks)
+    up, down, marks = gather(n, up, down, ends, (h,))
     ups.append(up)
     downs.append(down)
 

time: 279 us -> 278 us (level)
  transfers between devices with their start and end apart: 20 -> 20, of which waited for: 8 -> 9; matrix products, arithmetic and copies ran while one was open for 2% -> 2% of each run, Pallas kernels for 36% -> 36%
where the time goes in v3:
time: 278 us; the launch traced here: 277 us
  waiting for transfers between devices  130 us (47%)
  Pallas kernels  99.3 us (36%)
  starting transfers between devices  20.2 us (7%)
  between operations  14 us (5%)
  local copies, waits for them, and re-layouts  13.5 us (5%)
    ppermute x17, waiting for transfers between devices, exchange(): return lax.ppermute(a, 'fsdp', [(i, i ^ bit) for i in range(n)])  130 us
    pallas_call x2, Pallas kernels, forward(): pl.pallas_call(functools.partial(forward_kernel, n, first, half, resumed)...  44.7 us
    pallas_call x4, Pallas kernels, grads(): pl.pallas_call(functools.partial(grad_kernel, n, start + at, per_step, ha...  43 us
    ppermute x17, starting transfers between devices, exchange(): return lax.ppermute(a, 'fsdp', [(i, i ^ bit) for i in range(n)])  20.1 us
    pallas_call x4, Pallas kernels, finish(): pl.pallas_call(functools.partial(finish_kernel, len(got)), grid=(per_chun...  11.6 us
    unnamed x35, local copies, waits for them, and re-layouts  7.55 us
  transfers between devices with their start and end apart: 20, of which 9 were waited for; matrix products, arithmetic and copies ran while one was open for 2% of the time, Pallas kernels for 36%

profile of v3, /device:TPU:0, one launch (start us, length us, event | category | flops | bytes accessed | tf_op | source)
XLA Modules:
  0.0 277.3 jit_solution(13445362189682211162)
XLA Ops:
  8.2 1.0 constant_dynamic-update-slice_fusion
  10.3 1.8 fusion.1
  12.1 3.0 %collective-permute-start.1 = (bf16[16,2,128,128]{3,2,1,0:T(8,128)(2,1)S(1)}, bf16[16,2,128,128]{3,2,1,0:T(8,128)(2,1)}, u32[]{:S(2)}, u32[]{:S(2)}) collective-permute-start(bf16[16,2,128,128]{3,2,1,0:T(8,128)(2,1)S(1)} %get-tuple-element.89.refs_0_), channel_id=1, source_target_pairs={{0,8},{8,0},{16,24},{24,16},{1,9},{9,1},{17,25},{25,17},{2,10},{10... | collective-permute-start | bytes 3145736 | tf_op jit(solution)/shard_map/ppermute | solution.py:335
  15.1 1.1 fusion
  16.2 1.5 collective-permute-start.2
  18.7 1.6 collective-permute-start
  20.3 57.4 %collective-permute-done = bf16[24,16384]{1,0:T(8,128)(2,1)} collective-permute-done((bf16[24,16384]{1,0:T(8,128)(2,1)S(1)}, bf16[24,16384]{1,0:T(8,128)(2,1)}, u32[]{:S(2)}, u32[]{:S(2)}) %collective-permute-start) | collective-permute-done | bytes 786464 | tf_op jit(solution)/shard_map/ppermute | solution.py:335
  77.8 1.8 collective-permute-start.7
  79.6 1.5 collective-permute-start.8
  82.0 22.2 %collective-permute-done.7.refs_3_ = bf16[16,2,128,128]{3,2,1,0:T(8,128)(2,1)S(1)} collective-permute-done((bf16[16,2,128,128]{3,2,1,0:T(8,128)(2,1)}, bf16[16,2,128,128]{3,2,1,0:T(8,128)(2,1)S(1)}, u32[]{:S(2)}, u32[]{:S(2)}) %collective-permute-start.7) | collective-permute-done | bytes 1048608 | tf_op jit(solution)/shard_map/ppermute | solution.py:335
  104.2 1.8 collective-permute-done.8.refs_7_
  106.0 1.0 collective-permute-start.9
  107.0 1.5 collective-permute-start.10
  109.9 22.6 %forward_first.1 = (bf16[2,16,192,128]{3,2,1,0:T(8,128)(2,1)}, f32[192,16384]{1,0:T(8,128)}) custom-call(s32[1]{0:T(128)} %bitcast.me_ref, s32[32,8]{1,0:T(8,128)} %copy.22.up_idx, s32[32,8]{1,0:T(8,128)} %copy.23.down_idx, bf16[192,16384]{1,0:T(8,128)(2,1)} %all-gather.3.cloned.1.call-done.rows.mine_hbm, bf16[16,2,128,128]{3,2,1,0:T(8,128)(2,1)} %copy-done.2, ...), custom_call_target="tpu_custom_call" | custom-call | bytes 73800000 | tf_op jit(solution)/shard_map/forward_first/pallas_call | solution.py:247
  132.5 15.0 %collective-permute-done.9.refs_3_.refs_2_ = bf16[16,2,128,128]{3,2,1,0:T(8,128)(2,1)} collective-permute-done((bf16[16,2,128,128]{3,2,1,0:T(8,128)(2,1)S(1)}, bf16[16,2,128,128]{3,2,1,0:T(8,128)(2,1)}, u32[]{:S(2)}, u32[]{:S(2)}) %collective-permute-start.9) | collective-permute-done | bytes 1048608 | tf_op jit(solution)/shard_map/ppermute | solution.py:335
  147.5 1.2 collective-permute-done.10.refs_6_.refs_5_
  149.2 1.4 collective-permute-start.12
  150.7 10.7 %grad_chunk.4 = (f32[8,2,128,128]{3,2,1,0:T(8,128)}, f32[8,2,128,128]{3,2,1,0:T(8,128)}, bf16[2,8,2,128,128]{4,3,2,1,0:T(8,128)(2,1)}) custom-call(s32[1]{0:T(128)} %bitcast.me_ref, s32[32,8]{1,0:T(8,128)} %copy.22.up_idx, s32[32,8]{1,0:T(8,128)} %copy.23.down_idx, bf16[192,16384]{1,0:T(8,128)(2,1)} %all-gather.3.cloned.1.call-done.rows.mine_hbm, ...), custom_call_target="tpu_custom_call" | custom-call | bytes 44280000 | tf_op jit(solution)/shard_map/grad_chunk/pallas_call | solution.py:290
  161.3 1.6 collective-permute-start.13
  162.9 10.7 %grad_chunk.5 = (f32[8,2,128,128]{3,2,1,0:T(8,128)}, f32[8,2,128,128]{3,2,1,0:T(8,128)}, bf16[2,8,2,128,128]{4,3,2,1,0:T(8,128)(2,1)}) custom-call(s32[1]{0:T(128)} %bitcast.me_ref, s32[32,8]{1,0:T(8,128)} %copy.22.up_idx, s32[32,8]{1,0:T(8,128)} %copy.23.down_idx, bf16[192,16384]{1,0:T(8,128)(2,1)} %all-gather.3.cloned.1.call-done.rows.mine_hbm, ...), custom_call_target="tpu_custom_call" | custom-call | bytes 44280000 | tf_op jit(solution)/shard_map/grad_chunk/pallas_call | solution.py:290
  173.6 1.3 collective-permute-done.11.refs_4_.refs_3_
  176.3 22.1 %forward_last.1 = (bf16[2,16,192,128]{3,2,1,0:T(8,128)(2,1)}, bf16[192,16384]{1,0:T(8,128)(2,1)}) custom-call(s32[1]{0:T(128)} %bitcast.me_ref, s32[32,8]{1,0:T(8,128)} %copy.22.up_idx, s32[32,8]{1,0:T(8,128)} %copy.23.down_idx, bf16[192,16384]{1,0:T(8,128)(2,1)} %all-gather.3.cloned.1.call-done.rows.mine_hbm, f32[192,16384]{1,0:T(8,128)} %get-tuple-element.56.refs_0_, ...), custom_call_target="tpu_custom_call" | custom-call | bytes 73800000 | tf_op jit(solution)/shard_map/forward_last/pallas_call | solution.py:247
  199.0 10.9 %grad_chunk.6 = (f32[8,2,128,128]{3,2,1,0:T(8,128)}, f32[8,2,128,128]{3,2,1,0:T(8,128)}, bf16[2,8,2,128,128]{4,3,2,1,0:T(8,128)(2,1)}) custom-call(s32[1]{0:T(128)} %bitcast.me_ref, s32[32,8]{1,0:T(8,128)} %copy.22.up_idx, s32[32,8]{1,0:T(8,128)} %copy.23.down_idx, bf16[192,16384]{1,0:T(8,128)(2,1)} %all-gather.3.cloned.1.call-done.rows.mine_hbm, ...), custom_call_target="tpu_custom_call" | custom-call | bytes 44280000 | tf_op jit(solution)/shard_map/grad_chunk/pallas_call | solution.py:290
  209.9 1.6 collective-permute-start.15
  211.5 10.8 %grad_chunk.7 = (f32[8,2,128,128]{3,2,1,0:T(8,128)}, f32[8,2,128,128]{3,2,1,0:T(8,128)}, bf16[2,8,2,128,128]{4,3,2,1,0:T(8,128)(2,1)}) custom-call(s32[1]{0:T(128)} %bitcast.me_ref, s32[32,8]{1,0:T(8,128)} %copy.22.up_idx, s32[32,8]{1,0:T(8,128)} %copy.23.down_idx, bf16[192,16384]{1,0:T(8,128)(2,1)} %all-gather.3.cloned.1.call-done.rows.mine_hbm, ...), custom_call_target="tpu_custom_call" | custom-call | bytes 44280000 | tf_op jit(solution)/shard_map/grad_chunk/pallas_call | solution.py:290
  222.9 2.9 %finish_chunk.4 = (f32[32,2,128,128]{3,2,1,0:T(8,128)}, f32[32,2,128,128]{3,2,1,0:T(8,128)}) custom-call(f32[8,2,128,128]{3,2,1,0:T(8,128)} %get-tuple-element.76.own_up, f32[8,2,128,128]{3,2,1,0:T(8,128)} %get-tuple-element.77.own_down, bf16[2,8,2,128,128]{4,3,2,1,0:T(8,128)(2,1)} %copy-done.10), custom_call_target="tpu_custom_call" | custom-call | bytes 11070000 | tf_op jit(solution)/shard_map/finish_chunk/pallas_call | solution.py:317
  226.7 2.9 %finish_chunk.5 = (f32[32,2,128,128]{3,2,1,0:T(8,128)}, f32[32,2,128,128]{3,2,1,0:T(8,128)}) custom-call(f32[8,2,128,128]{3,2,1,0:T(8,128)} %get-tuple-element.73.own_up, f32[8,2,128,128]{3,2,1,0:T(8,128)} %get-tuple-element.74.own_down, bf16[2,8,2,128,128]{4,3,2,1,0:T(8,128)(2,1)} %copy-done.12, ...), custom_call_target="tpu_custom_call", output_to_operand_aliasing={{0}: (3, {}), {1}: (4, {})} | custom-call | bytes 11070000 | tf_op jit(solution)/shard_map/finish_chunk/pallas_call | solution.py:317
  229.6 17.7 %collective-permute-done.15.refs_0_ = bf16[2,8,2,128,128]{4,3,2,1,0:T(8,128)(2,1)S(1)} collective-permute-done((bf16[2,8,2,128,128]{4,3,2,1,0:T(8,128)(2,1)}, bf16[2,8,2,128,128]{4,3,2,1,0:T(8,128)(2,1)S(1)}, u32[]{:S(2)}, u32[]{:S(2)}) %collective-permute-start.15) | collective-permute-done | bytes 1048608 | tf_op jit(solution)/shard_map/ppermute | solution.py:335
  248.3 2.9 %finish_chunk.6 = (f32[32,2,128,128]{3,2,1,0:T(8,128)}, f32[32,2,128,128]{3,2,1,0:T(8,128)}) custom-call(f32[8,2,128,128]{3,2,1,0:T(8,128)} %get-tuple-element.70.own_up, f32[8,2,128,128]{3,2,1,0:T(8,128)} %get-tuple-element.71.own_down, bf16[2,8,2,128,128]{4,3,2,1,0:T(8,128)(2,1)} %copy-done.11, ...), custom_call_target="tpu_custom_call", output_to_operand_aliasing={{0}: (3, {}), {1}: (4, {})} | custom-call | bytes 11070000 | tf_op jit(solution)/shard_map/finish_chunk/pallas_call | solution.py:317
  251.2 13.1 %collective-permute-done.14.refs_0_ = bf16[2,8,2,128,128]{4,3,2,1,0:T(8,128)(2,1)S(1)} collective-permute-done((bf16[2,8,2,128,128]{4,3,2,1,0:T(8,128)(2,1)}, bf16[2,8,2,128,128]{4,3,2,1,0:T(8,128)(2,1)S(1)}, u32[]{:S(2)}, u32[]{:S(2)}) %collective-permute-start.14) | collective-permute-done | bytes 1048608 | tf_op jit(solution)/shard_map/ppermute | solution.py:335
  265.2 2.9 %finish_chunk.7 = (f32[32,2,128,128]{3,2,1,0:T(8,128)}, f32[32,2,128,128]{3,2,1,0:T(8,128)}) custom-call(f32[8,2,128,128]{3,2,1,0:T(8,128)} %get-tuple-element.67.own_up, f32[8,2,128,128]{3,2,1,0:T(8,128)} %get-tuple-element.68.own_down, bf16[2,8,2,128,128]{4,3,2,1,0:T(8,128)(2,1)} %copy-done.13, ...), custom_call_target="tpu_custom_call", output_to_operand_aliasing={{0}: (3, {}), {1}: (4, {})} | custom-call | bytes 11070000 | tf_op jit(solution)/shard_map/finish_chunk/pallas_call | solution.py:317
  268.7 2.0 fusion.2
  (60 shorter events, 11.8 us)
Async XLA Ops:
  7.2 102.7 %all-gather.3.cloned.1.call-start = ((), (), s32[]{:S(2)}) async-start(), calls=%async_computation.1 | async-start | bytes 7077888 | tf_op jit(solution)/shard_map/all_gather | solution.py:361
  10.2 98.3 %copy-start.14 = (s32[32,8]{0,1:T(8,128)S(1)}, s32[32,8]{0,1:T(8,128)}, u32[]{:S(2)}) copy-start(s32[32,8]{0,1:T(8,128)} %param.10) | copy-start | bytes 3076
  10.2 99.0 %copy-start.15 = (s32[32,8]{0,1:T(8,128)S(1)}, s32[32,8]{0,1:T(8,128)}, u32[]{:S(2)}) copy-start(s32[32,8]{0,1:T(8,128)} %param.11) | copy-start | bytes 3076
  10.2 140.5 %all-gather.5.cloned.1.call-start = ((), (), s32[]{:S(2)}) async-start(), calls=%async_computation.2 | async-start | bytes 7077888 | tf_op jit(solution)/shard_map/all_gather | solution.py:370
  10.2 4.9 %copy-start.7 = (bf16[32,2,128,128]{3,2,1,0:T(8,128)(2,1)S(1)}, bf16[32,2,128,128]{3,2,1,0:T(8,128)(2,1)}, u32[]{:S(2)}) copy-start(bf16[32,2,128,128]{3,2,1,0:T(8,128)(2,1)} %param.9) | copy-start | bytes 6291460
  10.3 8.5 %copy-start.9 = (bf16[24,16384]{1,0:T(8,128)(2,1)S(1)}, bf16[24,16384]{1,0:T(8,128)(2,1)}, u32[]{:S(2)}) copy-start(bf16[24,16384]{1,0:T(8,128)(2,1)} %copy-done.8) | copy-start | bytes 2359300
  12.1 97.8 %copy-start.2 = (bf16[16,2,128,128]{3,2,1,0:T(8,128)(2,1)}, bf16[16,2,128,128]{3,2,1,0:T(8,128)(2,1)S(1)}, u32[]{:S(2)}) copy-start(bf16[16,2,128,128]{3,2,1,0:T(8,128)(2,1)S(1)} %get-tuple-element.89.refs_0_) | copy-start | bytes 3145732
  12.1 120.3 %copy-start = (bf16[16,2,128,128]{3,2,1,0:T(8,128)(2,1)}, bf16[16,2,128,128]{3,2,1,0:T(8,128)(2,1)S(1)}, u32[]{:S(2)}) copy-start(bf16[16,2,128,128]{3,2,1,0:T(8,128)(2,1)S(1)} %get-tuple-element.48.refs_1_.refs_0_) | copy-start | bytes 3145732
  12.1 65.6 %collective-permute-start.1 = (bf16[16,2,128,128]{3,2,1,0:T(8,128)(2,1)S(1)}, bf16[16,2,128,128]{3,2,1,0:T(8,128)(2,1)}, u32[]{:S(2)}, u32[]{:S(2)}) collective-permute-start(bf16[16,2,128,128]{3,2,1,0:T(8,128)(2,1)S(1)} %get-tuple-element.89.refs_0_), channel_id=1, source_target_pairs={{0,8},{8,0},{16,24},{24,16},{1,9},{9,1},{17,25},{25,17},{2,10},{10... | collective-permute-start | bytes 3145736 | tf_op jit(solution)/shard_map/ppermute | solution.py:335
  16.2 116.2 %copy-start.1 = (bf16[16,2,128,128]{3,2,1,0:T(8,128)(2,1)}, bf16[16,2,128,128]{3,2,1,0:T(8,128)(2,1)S(1)}, u32[]{:S(2)}) copy-start(bf16[16,2,128,128]{3,2,1,0:T(8,128)(2,1)S(1)} %get-tuple-element.49.refs_5_.refs_4_) | copy-start | bytes 3145732
  16.2 61.5 %collective-permute-start.2 = (bf16[16,2,128,128]{3,2,1,0:T(8,128)(2,1)}, bf16[16,2,128,128]{3,2,1,0:T(8,128)(2,1)}, u32[]{:S(2)}, u32[]{:S(2)}) collective-permute-start(bf16[16,2,128,128]{3,2,1,0:T(8,128)(2,1)} %get-tuple-element.87.refs_4_), channel_id=1, source_target_pairs={{0,16},{8,24},{16,0},{24,8},{1,17},{9,25},{17,1},{25,9},{2,18},{10... | collective-permute-start | bytes 3145736 | tf_op jit(solution)/shard_map/ppermute | solution.py:335
  17.8 60.0 %collective-permute-start.3 = (bf16[16,2,128,128]{3,2,1,0:T(8,128)(2,1)S(1)}, bf16[16,2,128,128]{3,2,1,0:T(8,128)(2,1)}, u32[]{:S(2)}, u32[]{:S(2)}) collective-permute-start(bf16[16,2,128,128]{3,2,1,0:T(8,128)(2,1)S(1)} %get-tuple-element.89.refs_0_), channel_id=1, source_target_pairs={{0,16},{8,24},{16,0},{24,8},{1,17},{9,25},{17,1},{25,9},{2,18},{10... | collective-permute-start | bytes 3145736 | tf_op jit(solution)/shard_map/ppermute | solution.py:335
  18.3 59.5 %collective-permute-start.4 = (bf16[16,2,128,128]{3,2,1,0:T(8,128)(2,1)}, bf16[16,2,128,128]{3,2,1,0:T(8,128)(2,1)}, u32[]{:S(2)}, u32[]{:S(2)}) collective-permute-start(bf16[16,2,128,128]{3,2,1,0:T(8,128)(2,1)} %get-tuple-element.87.refs_4_), channel_id=1, source_target_pairs={{0,8},{8,0},{16,24},{24,16},{1,9},{9,1},{17,25},{25,17},{2,10},{10... | collective-permute-start | bytes 3145736 | tf_op jit(solution)/shard_map/ppermute | solution.py:335
  18.7 59.0 %collective-permute-start = (bf16[24,16384]{1,0:T(8,128)(2,1)S(1)}, bf16[24,16384]{1,0:T(8,128)(2,1)}, u32[]{:S(2)}, u32[]{:S(2)}) collective-permute-start(bf16[24,16384]{1,0:T(8,128)(2,1)S(1)} %copy-done.9), channel_id=1, source_target_pairs={{0,8},{8,0},{16,24},{24,16},{1,9},{9,1},{17,25},{25,17},{2,10},{10... | collective-permute-start | bytes 2359304 | tf_op jit(solution)/shard_map/ppermute | solution.py:335
  77.8 190.9 %reduce-scatter.2.cloned.1.call-start = ((), (), s32[]{:S(2)}) async-start(), calls=%async_computation.3 | async-start | bytes 7077888 | tf_op jit(solution)/shard_map/reduce_scatter | solution.py:392
  77.8 26.4 %collective-permute-start.7 = (bf16[16,2,128,128]{3,2,1,0:T(8,128)(2,1)}, bf16[16,2,128,128]{3,2,1,0:T(8,128)(2,1)S(1)}, u32[]{:S(2)}, u32[]{:S(2)}) collective-permute-start(bf16[16,2,128,128]{3,2,1,0:T(8,128)(2,1)} %collective-permute-done.1.refs_1_), channel_id=1, source_target_pairs={{0,16},{8,24},{16,0},{24,8},{1,17},{9,25},{17,1},{25,9},{2,18},{10... | collective-permute-start | bytes 3145736 | tf_op jit(solution)/shard_map/ppermute | solution.py:335
  79.6 26.3 %collective-permute-start.8 = (bf16[16,2,128,128]{3,2,1,0:T(8,128)(2,1)}, bf16[16,2,128,128]{3,2,1,0:T(8,128)(2,1)S(1)}, u32[]{:S(2)}, u32[]{:S(2)}) collective-permute-start(bf16[16,2,128,128]{3,2,1,0:T(8,128)(2,1)} %collective-permute-done.2.refs_6_), channel_id=1, source_target_pairs={{0,8},{8,0},{16,24},{24,16},{1,9},{9,1},{17,25},{25,17},{2,10},{10... | collective-permute-start | bytes 3145736 | tf_op jit(solution)/shard_map/ppermute | solution.py:335
  81.1 51.3 %collective-permute-start.5 = (bf16[16,2,128,128]{3,2,1,0:T(8,128)(2,1)S(1)}, bf16[16,2,128,128]{3,2,1,0:T(8,128)(2,1)}, u32[]{:S(2)}, u32[]{:S(2)}) collective-permute-start(bf16[16,2,128,128]{3,2,1,0:T(8,128)(2,1)S(1)} %get-tuple-element.48.refs_1_.refs_0_), channel_id=1, source_target_pairs={{0,8},{8,0},{16,24},{24,16},{1,9},{9,1},{17,25},{25,17},{2,10},{10... | collective-permute-start | bytes 3145736 | tf_op jit(solution)/shard_map/ppermute | solution.py:335
  81.7 50.8 %collective-permute-start.6 = (bf16[16,2,128,128]{3,2,1,0:T(8,128)(2,1)S(1)}, bf16[16,2,128,128]{3,2,1,0:T(8,128)(2,1)}, u32[]{:S(2)}, u32[]{:S(2)}) collective-permute-start(bf16[16,2,128,128]{3,2,1,0:T(8,128)(2,1)S(1)} %get-tuple-element.49.refs_5_.refs_4_), channel_id=1, source_target_pairs={{0,16},{8,24},{16,0},{24,8},{1,17},{9,25},{17,1},{25,9},{2,18},{10... | collective-permute-start | bytes 3145736 | tf_op jit(solution)/shard_map/ppermute | solution.py:335
  104.2 1.8 copy-start.3
  106.0 1.0 copy-start.4
  106.0 41.5 %collective-permute-start.9 = (bf16[16,2,128,128]{3,2,1,0:T(8,128)(2,1)S(1)}, bf16[16,2,128,128]{3,2,1,0:T(8,128)(2,1)}, u32[]{:S(2)}, u32[]{:S(2)}) collective-permute-start(bf16[16,2,128,128]{3,2,1,0:T(8,128)(2,1)S(1)} %get-tuple-element.48.refs_1_.refs_0_), channel_id=1, source_target_pairs={{0,16},{8,24},{16,0},{24,8},{1,17},{9,25},{17,1},{25,9},{2,18},{10... | collective-permute-start | bytes 3145736 | tf_op jit(solution)/shard_map/ppermute | solution.py:335
  107.0 41.7 %collective-permute-start.10 = (bf16[16,2,128,128]{3,2,1,0:T(8,128)(2,1)S(1)}, bf16[16,2,128,128]{3,2,1,0:T(8,128)(2,1)}, u32[]{:S(2)}, u32[]{:S(2)}) collective-permute-start(bf16[16,2,128,128]{3,2,1,0:T(8,128)(2,1)S(1)} %get-tuple-element.49.refs_5_.refs_4_), channel_id=1, source_target_pairs={{0,8},{8,0},{16,24},{24,16},{1,9},{9,1},{17,25},{25,17},{2,10},{10... | collective-permute-start | bytes 3145736 | tf_op jit(solution)/shard_map/ppermute | solution.py:335
  148.7 26.3 %collective-permute-start.11 = (bf16[16,2,128,128]{3,2,1,0:T(8,128)(2,1)}, bf16[16,2,128,128]{3,2,1,0:T(8,128)(2,1)S(1)}, u32[]{:S(2)}, u32[]{:S(2)}) collective-permute-start(bf16[16,2,128,128]{3,2,1,0:T(8,128)(2,1)} %collective-permute-done.5.refs_2_.refs_1_), channel_id=1, source_target_pairs={{0,16},{8,24},{16,0},{24,8},{1,17},{9,25},{17,1},{25,9},{2,18},{10... | collective-permute-start | bytes 3145736 | tf_op jit(solution)/shard_map/ppermute | solution.py:335
  149.2 25.7 %collective-permute-start.12 = (bf16[16,2,128,128]{3,2,1,0:T(8,128)(2,1)}, bf16[16,2,128,128]{3,2,1,0:T(8,128)(2,1)S(1)}, u32[]{:S(2)}, u32[]{:S(2)}) collective-permute-start(bf16[16,2,128,128]{3,2,1,0:T(8,128)(2,1)} %collective-permute-done.6.refs_7_.refs_6_), channel_id=1, source_target_pairs={{0,8},{8,0},{16,24},{24,16},{1,9},{9,1},{17,25},{25,17},{2,10},{10... | collective-permute-start | bytes 3145736 | tf_op jit(solution)/shard_map/ppermute | solution.py:335
  161.3 37.1 %collective-permute-start.13 = (bf16[2,8,2,128,128]{4,3,2,1,0:T(8,128)(2,1)}, bf16[2,8,2,128,128]{4,3,2,1,0:T(8,128)(2,1)S(1)}, u32[]{:S(2)}, u32[]{:S(2)}) collective-permute-start(bf16[2,8,2,128,128]{4,3,2,1,0:T(8,128)(2,1)} %get-tuple-element.52), channel_id=1, source_target_pairs={{0,16},{8,24},{16,0},{24,8},{1,17},{9,25},{17,1},{25,9},{2,18},{10... | collective-permute-start | bytes 3145736 | tf_op jit(solution)/shard_map/ppermute | solution.py:335
  175.0 1.3 copy-start.6
  198.4 11.5 %copy-start.10 = (bf16[2,8,2,128,128]{4,3,2,1,0:T(8,128)(2,1)}, bf16[2,8,2,128,128]{4,3,2,1,0:T(8,128)(2,1)S(1)}, u32[]{:S(2)}) copy-start(bf16[2,8,2,128,128]{4,3,2,1,0:T(8,128)(2,1)S(1)} %collective-permute-done.13.refs_0_) | copy-start | bytes 3145732
  198.4 27.3 %collective-permute-start.16 = (bf16[2,8,2,128,128]{4,3,2,1,0:T(8,128)(2,1)}, bf16[2,8,2,128,128]{4,3,2,1,0:T(8,128)(2,1)S(1)}, u32[]{:S(2)}, u32[]{:S(2)}) collective-permute-start(bf16[2,8,2,128,128]{4,3,2,1,0:T(8,128)(2,1)} %get-tuple-element.54), channel_id=1, source_target_pairs={{0,16},{8,24},{16,0},{24,8},{1,17},{9,25},{17,1},{25,9},{2,18},{10... | collective-permute-start | bytes 3145736 | tf_op jit(solution)/shard_map/ppermute | solution.py:335
  209.9 37.4 %collective-permute-start.15 = (bf16[2,8,2,128,128]{4,3,2,1,0:T(8,128)(2,1)}, bf16[2,8,2,128,128]{4,3,2,1,0:T(8,128)(2,1)S(1)}, u32[]{:S(2)}, u32[]{:S(2)}) collective-permute-start(bf16[2,8,2,128,128]{4,3,2,1,0:T(8,128)(2,1)} %get-tuple-element.63), channel_id=1, source_target_pairs={{0,16},{8,24},{16,0},{24,8},{1,17},{9,25},{17,1},{25,9},{2,18},{10... | collective-permute-start | bytes 3145736 | tf_op jit(solution)/shard_map/ppermute | solution.py:335
  222.3 42.0 %collective-permute-start.14 = (bf16[2,8,2,128,128]{4,3,2,1,0:T(8,128)(2,1)}, bf16[2,8,2,128,128]{4,3,2,1,0:T(8,128)(2,1)S(1)}, u32[]{:S(2)}, u32[]{:S(2)}) collective-permute-start(bf16[2,8,2,128,128]{4,3,2,1,0:T(8,128)(2,1)} %get-tuple-element.66), channel_id=1, source_target_pairs={{0,16},{8,24},{16,0},{24,8},{1,17},{9,25},{17,1},{25,9},{2,18},{10... | collective-permute-start | bytes 3145736 | tf_op jit(solution)/shard_map/ppermute | solution.py:335
  247.3 1.0 copy-start.11
  (4 other events, 3.8 us)
Sparse Core Ops, SparseCore 0:
  10.3 67.4 all-gather.2
  79.4 64.7 all-gather.4
  198.6 70.0 reduce-scatter.1

commit v4 on v3

--- a/solution.py
+++ b/solution.py
@@ -377,16 +377,20 @@
     ups.append(up)
     downs.append(down)
 
+    def swap(sent):
+        return [exchange(part, 2 * (e + 1), n) for e, part in enumerate(sent)]
+
     def grad_chunk(c, *earlier):
         g, at = c * per_chunk // per_group, c * per_chunk % per_group
         rows = after(other, *earlier)
         up, down, *sent = grads(
             n, g * per_group, at, per_chunk, me, up_index, down_index, mine, rows, hs[g], ups[g], downs[g]
         )
-        return up, down, sent, [exchange(part, 2 * (e + 1), n) for e, part in enumerate(sent)]
+        return up, down, sent, [] if c == 0 else swap(sent)
 
     parts = [grad_chunk(0, *marks)]
     parts.append(grad_chunk(1, *parts[0][2]))
+    parts[0][3].extend(swap([after(part, *parts[1][2]) for part in parts[0][2]]))
     h, total = forward_group(1, after(mine, *parts[1][2]), partial)
     hs.append(h)
     sums = lax.psum_scatter(after(total, *parts[0][3]), "tensor", scatter_dimension=0, tiled=True)

time: 278 us -> 277 us (level)
  transfers between devices with their start and end apart: 20 -> 20, of which waited for: 9 -> 7; matrix products, arithmetic and copies ran while one was open for 2% -> 2% of each run, Pallas kernels for 36% -> 36%
where the time goes in v4:
time: 277 us
  waiting for transfers between devices  130 us (47%)
  Pallas kernels  99.5 us (36%)
  starting transfers between devices  20.2 us (7%)
  between operations  14 us (5%)
  local copies, waits for them, and re-layouts  13.5 us (5%)
    ppermute x17, waiting for transfers between devices, exchange(): return lax.ppermute(a, 'fsdp', [(i, i ^ bit) for i in range(n)])  130 us
    pallas_call x2, Pallas kernels, forward(): pl.pallas_call(functools.partial(forward_kernel, n, first, half, resumed)...  44.7 us
    pallas_call x4, Pallas kernels, grads(): pl.pallas_call(functools.partial(grad_kernel, n, start + at, per_step, ha...  43 us
    ppermute x17, starting transfers between devices, exchange(): return lax.ppermute(a, 'fsdp', [(i, i ^ bit) for i in range(n)])  20 us
    pallas_call x4, Pallas kernels, finish(): pl.pallas_call(functools.partial(finish_kernel, len(got)), grid=(per_chun...  11.8 us
    unnamed x35, local copies, waits for them, and re-layouts  7.54 us
  transfers between devices with their start and end apart: 20, of which 7 were waited for; matrix products, arithmetic and copies ran while one was open for 2% of the time, Pallas kernels for 36%

profile of v4, /device:TPU:0, one launch (start us, length us, event | category | flops | bytes accessed | tf_op | source)
XLA Modules:
  0.0 276.8 jit_solution(10162101964948239217)
XLA Ops:
  7.2 1.0 constant_dynamic-update-slice_fusion.1
  8.2 1.0 constant_dynamic-update-slice_fusion
  10.3 1.8 fusion.1
  12.1 3.0 %collective-permute-start.1 = (bf16[16,2,128,128]{3,2,1,0:T(8,128)(2,1)S(1)}, bf16[16,2,128,128]{3,2,1,0:T(8,128)(2,1)}, u32[]{:S(2)}, u32[]{:S(2)}) collective-permute-start(bf16[16,2,128,128]{3,2,1,0:T(8,128)(2,1)S(1)} %get-tuple-element.91.refs_0_), channel_id=1, source_target_pairs={{0,8},{8,0},{16,24},{24,16},{1,9},{9,1},{17,25},{25,17},{2,10},{10... | collective-permute-start | bytes 3145736 | tf_op jit(solution)/shard_map/ppermute | solution.py:335
  15.1 1.1 fusion
  16.2 1.5 collective-permute-start.2
  18.7 1.6 collective-permute-start
  20.3 57.4 %collective-permute-done = bf16[24,16384]{1,0:T(8,128)(2,1)} collective-permute-done((bf16[24,16384]{1,0:T(8,128)(2,1)S(1)}, bf16[24,16384]{1,0:T(8,128)(2,1)}, u32[]{:S(2)}, u32[]{:S(2)}) %collective-permute-start) | collective-permute-done | bytes 786464 | tf_op jit(solution)/shard_map/ppermute | solution.py:335
  77.8 1.8 collective-permute-start.7
  79.6 1.5 collective-permute-start.8
  82.0 22.2 %collective-permute-done.7.refs_3_ = bf16[16,2,128,128]{3,2,1,0:T(8,128)(2,1)S(1)} collective-permute-done((bf16[16,2,128,128]{3,2,1,0:T(8,128)(2,1)}, bf16[16,2,128,128]{3,2,1,0:T(8,128)(2,1)S(1)}, u32[]{:S(2)}, u32[]{:S(2)}) %collective-permute-start.7) | collective-permute-done | bytes 1048608 | tf_op jit(solution)/shard_map/ppermute | solution.py:335
  104.2 1.8 collective-permute-done.8.refs_7_
  106.0 1.0 collective-permute-start.9
  107.0 1.5 collective-permute-start.10
  109.9 22.6 %forward_first.1 = (bf16[2,16,192,128]{3,2,1,0:T(8,128)(2,1)}, f32[192,16384]{1,0:T(8,128)}) custom-call(s32[1]{0:T(128)} %bitcast.me_ref, s32[32,8]{1,0:T(8,128)} %copy.22.up_idx, s32[32,8]{1,0:T(8,128)} %copy.23.down_idx, bf16[192,16384]{1,0:T(8,128)(2,1)} %all-gather.3.cloned.1.call-done.rows.mine_hbm, bf16[16,2,128,128]{3,2,1,0:T(8,128)(2,1)} %copy-done.2, ...), custom_call_target="tpu_custom_call" | custom-call | bytes 73800000 | tf_op jit(solution)/shard_map/forward_first/pallas_call | solution.py:247
  132.5 15.0 %collective-permute-done.9.refs_3_.refs_2_ = bf16[16,2,128,128]{3,2,1,0:T(8,128)(2,1)} collective-permute-done((bf16[16,2,128,128]{3,2,1,0:T(8,128)(2,1)S(1)}, bf16[16,2,128,128]{3,2,1,0:T(8,128)(2,1)}, u32[]{:S(2)}, u32[]{:S(2)}) %collective-permute-start.9) | collective-permute-done | bytes 1048608 | tf_op jit(solution)/shard_map/ppermute | solution.py:335
  147.5 1.2 collective-permute-done.10.refs_6_.refs_5_
  149.2 1.4 collective-permute-start.12
  150.7 10.6 %grad_chunk.4 = (f32[8,2,128,128]{3,2,1,0:T(8,128)}, f32[8,2,128,128]{3,2,1,0:T(8,128)}, bf16[2,8,2,128,128]{4,3,2,1,0:T(8,128)(2,1)}) custom-call(s32[1]{0:T(128)} %bitcast.me_ref, s32[32,8]{1,0:T(8,128)} %copy.22.up_idx, s32[32,8]{1,0:T(8,128)} %copy.23.down_idx, bf16[192,16384]{1,0:T(8,128)(2,1)} %all-gather.3.cloned.1.call-done.rows.mine_hbm, ...), custom_call_target="tpu_custom_call" | custom-call | bytes 44280000 | tf_op jit(solution)/shard_map/grad_chunk/pallas_call | solution.py:290
  161.3 10.7 %grad_chunk.5 = (f32[8,2,128,128]{3,2,1,0:T(8,128)}, f32[8,2,128,128]{3,2,1,0:T(8,128)}, bf16[2,8,2,128,128]{4,3,2,1,0:T(8,128)(2,1)}) custom-call(s32[1]{0:T(128)} %bitcast.me_ref, s32[32,8]{1,0:T(8,128)} %copy.22.up_idx, s32[32,8]{1,0:T(8,128)} %copy.23.down_idx, bf16[192,16384]{1,0:T(8,128)(2,1)} %all-gather.3.cloned.1.call-done.rows.mine_hbm, ...), custom_call_target="tpu_custom_call" | custom-call | bytes 44280000 | tf_op jit(solution)/shard_map/grad_chunk/pallas_call | solution.py:290
  172.0 1.6 collective-permute-start.13
  174.9 22.1 %forward_last.1 = (bf16[2,16,192,128]{3,2,1,0:T(8,128)(2,1)}, bf16[192,16384]{1,0:T(8,128)(2,1)}) custom-call(s32[1]{0:T(128)} %bitcast.me_ref, s32[32,8]{1,0:T(8,128)} %copy.22.up_idx, s32[32,8]{1,0:T(8,128)} %copy.23.down_idx, bf16[192,16384]{1,0:T(8,128)(2,1)} %all-gather.3.cloned.1.call-done.rows.mine_hbm, f32[192,16384]{1,0:T(8,128)} %get-tuple-element.57.refs_0_, ...), custom_call_target="tpu_custom_call" | custom-call | bytes 73800000 | tf_op jit(solution)/shard_map/forward_last/pallas_call | solution.py:247
  197.6 10.9 %grad_chunk.6 = (f32[8,2,128,128]{3,2,1,0:T(8,128)}, f32[8,2,128,128]{3,2,1,0:T(8,128)}, bf16[2,8,2,128,128]{4,3,2,1,0:T(8,128)(2,1)}) custom-call(s32[1]{0:T(128)} %bitcast.me_ref, s32[32,8]{1,0:T(8,128)} %copy.22.up_idx, s32[32,8]{1,0:T(8,128)} %copy.23.down_idx, bf16[192,16384]{1,0:T(8,128)(2,1)} %all-gather.3.cloned.1.call-done.rows.mine_hbm, ...), custom_call_target="tpu_custom_call" | custom-call | bytes 44280000 | tf_op jit(solution)/shard_map/grad_chunk/pallas_call | solution.py:290
  208.5 1.6 collective-permute-start.15
  210.1 10.7 %grad_chunk.7 = (f32[8,2,128,128]{3,2,1,0:T(8,128)}, f32[8,2,128,128]{3,2,1,0:T(8,128)}, bf16[2,8,2,128,128]{4,3,2,1,0:T(8,128)(2,1)}) custom-call(s32[1]{0:T(128)} %bitcast.me_ref, s32[32,8]{1,0:T(8,128)} %copy.22.up_idx, s32[32,8]{1,0:T(8,128)} %copy.23.down_idx, bf16[192,16384]{1,0:T(8,128)(2,1)} %all-gather.3.cloned.1.call-done.rows.mine_hbm, ...), custom_call_target="tpu_custom_call" | custom-call | bytes 44280000 | tf_op jit(solution)/shard_map/grad_chunk/pallas_call | solution.py:290
  221.4 2.9 %finish_chunk.4 = (f32[32,2,128,128]{3,2,1,0:T(8,128)}, f32[32,2,128,128]{3,2,1,0:T(8,128)}) custom-call(f32[8,2,128,128]{3,2,1,0:T(8,128)} %get-tuple-element.78.own_up, f32[8,2,128,128]{3,2,1,0:T(8,128)} %get-tuple-element.79.own_down, bf16[2,8,2,128,128]{4,3,2,1,0:T(8,128)(2,1)} %copy-done.10), custom_call_target="tpu_custom_call" | custom-call | bytes 11070000 | tf_op jit(solution)/shard_map/finish_chunk/pallas_call | solution.py:317
  225.4 2.9 %finish_chunk.5 = (f32[32,2,128,128]{3,2,1,0:T(8,128)}, f32[32,2,128,128]{3,2,1,0:T(8,128)}) custom-call(f32[8,2,128,128]{3,2,1,0:T(8,128)} %get-tuple-element.75.own_up, f32[8,2,128,128]{3,2,1,0:T(8,128)} %get-tuple-element.76.own_down, bf16[2,8,2,128,128]{4,3,2,1,0:T(8,128)(2,1)} %copy-done.12, ...), custom_call_target="tpu_custom_call", output_to_operand_aliasing={{0}: (3, {}), {1}: (4, {})} | custom-call | bytes 11070000 | tf_op jit(solution)/shard_map/finish_chunk/pallas_call | solution.py:317
  228.3 17.6 %collective-permute-done.15.refs_0_ = bf16[2,8,2,128,128]{4,3,2,1,0:T(8,128)(2,1)S(1)} collective-permute-done((bf16[2,8,2,128,128]{4,3,2,1,0:T(8,128)(2,1)}, bf16[2,8,2,128,128]{4,3,2,1,0:T(8,128)(2,1)S(1)}, u32[]{:S(2)}, u32[]{:S(2)}) %collective-permute-start.15) | collective-permute-done | bytes 1048608 | tf_op jit(solution)/shard_map/ppermute | solution.py:335
  246.9 2.9 %finish_chunk.6 = (f32[32,2,128,128]{3,2,1,0:T(8,128)}, f32[32,2,128,128]{3,2,1,0:T(8,128)}) custom-call(f32[8,2,128,128]{3,2,1,0:T(8,128)} %get-tuple-element.72.own_up, f32[8,2,128,128]{3,2,1,0:T(8,128)} %get-tuple-element.73.own_down, bf16[2,8,2,128,128]{4,3,2,1,0:T(8,128)(2,1)} %copy-done.11, ...), custom_call_target="tpu_custom_call", output_to_operand_aliasing={{0}: (3, {}), {1}: (4, {})} | custom-call | bytes 11070000 | tf_op jit(solution)/shard_map/finish_chunk/pallas_call | solution.py:317
  249.8 14.5 %collective-permute-done.14.refs_0_ = bf16[2,8,2,128,128]{4,3,2,1,0:T(8,128)(2,1)S(1)} collective-permute-done((bf16[2,8,2,128,128]{4,3,2,1,0:T(8,128)(2,1)}, bf16[2,8,2,128,128]{4,3,2,1,0:T(8,128)(2,1)S(1)}, u32[]{:S(2)}, u32[]{:S(2)}) %collective-permute-start.14) | collective-permute-done | bytes 1048608 | tf_op jit(solution)/shard_map/ppermute | solution.py:335
  265.3 3.0 %finish_chunk.7 = (f32[32,2,128,128]{3,2,1,0:T(8,128)}, f32[32,2,128,128]{3,2,1,0:T(8,128)}) custom-call(f32[8,2,128,128]{3,2,1,0:T(8,128)} %get-tuple-element.69.own_up, f32[8,2,128,128]{3,2,1,0:T(8,128)} %get-tuple-element.70.own_down, bf16[2,8,2,128,128]{4,3,2,1,0:T(8,128)(2,1)} %copy-done.13, ...), custom_call_target="tpu_custom_call", output_to_operand_aliasing={{0}: (3, {}), {1}: (4, {})} | custom-call | bytes 11070000 | tf_op jit(solution)/shard_map/finish_chunk/pallas_call | solution.py:317
  268.3 2.0 fusion.2
  (60 shorter events, 10.2 us)
Async XLA Ops:
  7.2 102.7 %all-gather.3.cloned.1.call-start = ((), (), s32[]{:S(2)}) async-start(), calls=%async_computation.1 | async-start | bytes 7077888 | tf_op jit(solution)/shard_map/all_gather | solution.py:361
  10.2 98.3 %copy-start.14 = (s32[32,8]{0,1:T(8,128)S(1)}, s32[32,8]{0,1:T(8,128)}, u32[]{:S(2)}) copy-start(s32[32,8]{0,1:T(8,128)} %param.10) | copy-start | bytes 3076
  10.2 99.0 %copy-start.15 = (s32[32,8]{0,1:T(8,128)S(1)}, s32[32,8]{0,1:T(8,128)}, u32[]{:S(2)}) copy-start(s32[32,8]{0,1:T(8,128)} %param.11) | copy-start | bytes 3076
  10.2 140.5 %all-gather.5.cloned.1.call-start = ((), (), s32[]{:S(2)}) async-start(), calls=%async_computation.2 | async-start | bytes 7077888 | tf_op jit(solution)/shard_map/all_gather | solution.py:370
  10.2 4.9 %copy-start.7 = (bf16[32,2,128,128]{3,2,1,0:T(8,128)(2,1)S(1)}, bf16[32,2,128,128]{3,2,1,0:T(8,128)(2,1)}, u32[]{:S(2)}) copy-start(bf16[32,2,128,128]{3,2,1,0:T(8,128)(2,1)} %param.9) | copy-start | bytes 6291460
  10.3 8.5 %copy-start.9 = (bf16[24,16384]{1,0:T(8,128)(2,1)S(1)}, bf16[24,16384]{1,0:T(8,128)(2,1)}, u32[]{:S(2)}) copy-start(bf16[24,16384]{1,0:T(8,128)(2,1)} %copy-done.8) | copy-start | bytes 2359300
  12.1 97.8 %copy-start.2 = (bf16[16,2,128,128]{3,2,1,0:T(8,128)(2,1)}, bf16[16,2,128,128]{3,2,1,0:T(8,128)(2,1)S(1)}, u32[]{:S(2)}) copy-start(bf16[16,2,128,128]{3,2,1,0:T(8,128)(2,1)S(1)} %get-tuple-element.91.refs_0_) | copy-start | bytes 3145732
  12.1 120.4 %copy-start = (bf16[16,2,128,128]{3,2,1,0:T(8,128)(2,1)}, bf16[16,2,128,128]{3,2,1,0:T(8,128)(2,1)S(1)}, u32[]{:S(2)}) copy-start(bf16[16,2,128,128]{3,2,1,0:T(8,128)(2,1)S(1)} %get-tuple-element.49.refs_1_.refs_0_) | copy-start | bytes 3145732
  12.1 65.6 %collective-permute-start.1 = (bf16[16,2,128,128]{3,2,1,0:T(8,128)(2,1)S(1)}, bf16[16,2,128,128]{3,2,1,0:T(8,128)(2,1)}, u32[]{:S(2)}, u32[]{:S(2)}) collective-permute-start(bf16[16,2,128,128]{3,2,1,0:T(8,128)(2,1)S(1)} %get-tuple-element.91.refs_0_), channel_id=1, source_target_pairs={{0,8},{8,0},{16,24},{24,16},{1,9},{9,1},{17,25},{25,17},{2,10},{10... | collective-permute-start | bytes 3145736 | tf_op jit(solution)/shard_map/ppermute | solution.py:335
  16.2 116.3 %copy-start.1 = (bf16[16,2,128,128]{3,2,1,0:T(8,128)(2,1)}, bf16[16,2,128,128]{3,2,1,0:T(8,128)(2,1)S(1)}, u32[]{:S(2)}) copy-start(bf16[16,2,128,128]{3,2,1,0:T(8,128)(2,1)S(1)} %get-tuple-element.50.refs_5_.refs_4_) | copy-start | bytes 3145732
  16.2 61.5 %collective-permute-start.2 = (bf16[16,2,128,128]{3,2,1,0:T(8,128)(2,1)}, bf16[16,2,128,128]{3,2,1,0:T(8,128)(2,1)}, u32[]{:S(2)}, u32[]{:S(2)}) collective-permute-start(bf16[16,2,128,128]{3,2,1,0:T(8,128)(2,1)} %get-tuple-element.89.refs_4_), channel_id=1, source_target_pairs={{0,16},{8,24},{16,0},{24,8},{1,17},{9,25},{17,1},{25,9},{2,18},{10... | collective-permute-start | bytes 3145736 | tf_op jit(solution)/shard_map/ppermute | solution.py:335
  17.8 60.0 %collective-permute-start.3 = (bf16[16,2,128,128]{3,2,1,0:T(8,128)(2,1)S(1)}, bf16[16,2,128,128]{3,2,1,0:T(8,128)(2,1)}, u32[]{:S(2)}, u32[]{:S(2)}) collective-permute-start(bf16[16,2,128,128]{3,2,1,0:T(8,128)(2,1)S(1)} %get-tuple-element.91.refs_0_), channel_id=1, source_target_pairs={{0,16},{8,24},{16,0},{24,8},{1,17},{9,25},{17,1},{25,9},{2,18},{10... | collective-permute-start | bytes 3145736 | tf_op jit(solution)/shard_map/ppermute | solution.py:335
  18.3 59.5 %collective-permute-start.4 = (bf16[16,2,128,128]{3,2,1,0:T(8,128)(2,1)}, bf16[16,2,128,128]{3,2,1,0:T(8,128)(2,1)}, u32[]{:S(2)}, u32[]{:S(2)}) collective-permute-start(bf16[16,2,128,128]{3,2,1,0:T(8,128)(2,1)} %get-tuple-element.89.refs_4_), channel_id=1, source_target_pairs={{0,8},{8,0},{16,24},{24,16},{1,9},{9,1},{17,25},{25,17},{2,10},{10... | collective-permute-start | bytes 3145736 | tf_op jit(solution)/shard_map/ppermute | solution.py:335
  18.7 59.0 %collective-permute-start = (bf16[24,16384]{1,0:T(8,128)(2,1)S(1)}, bf16[24,16384]{1,0:T(8,128)(2,1)}, u32[]{:S(2)}, u32[]{:S(2)}) collective-permute-start(bf16[24,16384]{1,0:T(8,128)(2,1)S(1)} %copy-done.9), channel_id=1, source_target_pairs={{0,8},{8,0},{16,24},{24,16},{1,9},{9,1},{17,25},{25,17},{2,10},{10... | collective-permute-start | bytes 2359304 | tf_op jit(solution)/shard_map/ppermute | solution.py:335
  77.8 190.5 %reduce-scatter.2.cloned.1.call-start = ((), (), s32[]{:S(2)}) async-start(), calls=%async_computation.3 | async-start | bytes 7077888 | tf_op jit(solution)/shard_map/reduce_scatter | solution.py:396
  77.8 26.4 %collective-permute-start.7 = (bf16[16,2,128,128]{3,2,1,0:T(8,128)(2,1)}, bf16[16,2,128,128]{3,2,1,0:T(8,128)(2,1)S(1)}, u32[]{:S(2)}, u32[]{:S(2)}) collective-permute-start(bf16[16,2,128,128]{3,2,1,0:T(8,128)(2,1)} %collective-permute-done.1.refs_1_), channel_id=1, source_target_pairs={{0,16},{8,24},{16,0},{24,8},{1,17},{9,25},{17,1},{25,9},{2,18},{10... | collective-permute-start | bytes 3145736 | tf_op jit(solution)/shard_map/ppermute | solution.py:335
  79.6 26.3 %collective-permute-start.8 = (bf16[16,2,128,128]{3,2,1,0:T(8,128)(2,1)}, bf16[16,2,128,128]{3,2,1,0:T(8,128)(2,1)S(1)}, u32[]{:S(2)}, u32[]{:S(2)}) collective-permute-start(bf16[16,2,128,128]{3,2,1,0:T(8,128)(2,1)} %collective-permute-done.2.refs_6_), channel_id=1, source_target_pairs={{0,8},{8,0},{16,24},{24,16},{1,9},{9,1},{17,25},{25,17},{2,10},{10... | collective-permute-start | bytes 3145736 | tf_op jit(solution)/shard_map/ppermute | solution.py:335
  81.1 51.4 %collective-permute-start.5 = (bf16[16,2,128,128]{3,2,1,0:T(8,128)(2,1)S(1)}, bf16[16,2,128,128]{3,2,1,0:T(8,128)(2,1)}, u32[]{:S(2)}, u32[]{:S(2)}) collective-permute-start(bf16[16,2,128,128]{3,2,1,0:T(8,128)(2,1)S(1)} %get-tuple-element.49.refs_1_.refs_0_), channel_id=1, source_target_pairs={{0,8},{8,0},{16,24},{24,16},{1,9},{9,1},{17,25},{25,17},{2,10},{10... | collective-permute-start | bytes 3145736 | tf_op jit(solution)/shard_map/ppermute | solution.py:335
  81.7 50.8 %collective-permute-start.6 = (bf16[16,2,128,128]{3,2,1,0:T(8,128)(2,1)S(1)}, bf16[16,2,128,128]{3,2,1,0:T(8,128)(2,1)}, u32[]{:S(2)}, u32[]{:S(2)}) collective-permute-start(bf16[16,2,128,128]{3,2,1,0:T(8,128)(2,1)S(1)} %get-tuple-element.50.refs_5_.refs_4_), channel_id=1, source_target_pairs={{0,16},{8,24},{16,0},{24,8},{1,17},{9,25},{17,1},{25,9},{2,18},{10... | collective-permute-start | bytes 3145736 | tf_op jit(solution)/shard_map/ppermute | solution.py:335
  104.2 1.8 copy-start.3
  106.0 1.0 copy-start.4
  106.0 41.5 %collective-permute-start.9 = (bf16[16,2,128,128]{3,2,1,0:T(8,128)(2,1)S(1)}, bf16[16,2,128,128]{3,2,1,0:T(8,128)(2,1)}, u32[]{:S(2)}, u32[]{:S(2)}) collective-permute-start(bf16[16,2,128,128]{3,2,1,0:T(8,128)(2,1)S(1)} %get-tuple-element.49.refs_1_.refs_0_), channel_id=1, source_target_pairs={{0,16},{8,24},{16,0},{24,8},{1,17},{9,25},{17,1},{25,9},{2,18},{10... | collective-permute-start | bytes 3145736 | tf_op jit(solution)/shard_map/ppermute | solution.py:335
  107.0 41.7 %collective-permute-start.10 = (bf16[16,2,128,128]{3,2,1,0:T(8,128)(2,1)S(1)}, bf16[16,2,128,128]{3,2,1,0:T(8,128)(2,1)}, u32[]{:S(2)}, u32[]{:S(2)}) collective-permute-start(bf16[16,2,128,128]{3,2,1,0:T(8,128)(2,1)S(1)} %get-tuple-element.50.refs_5_.refs_4_), channel_id=1, source_target_pairs={{0,8},{8,0},{16,24},{24,16},{1,9},{9,1},{17,25},{25,17},{2,10},{10... | collective-permute-start | bytes 3145736 | tf_op jit(solution)/shard_map/ppermute | solution.py:335
  148.7 25.0 %collective-permute-start.11 = (bf16[16,2,128,128]{3,2,1,0:T(8,128)(2,1)}, bf16[16,2,128,128]{3,2,1,0:T(8,128)(2,1)S(1)}, u32[]{:S(2)}, u32[]{:S(2)}) collective-permute-start(bf16[16,2,128,128]{3,2,1,0:T(8,128)(2,1)} %collective-permute-done.5.refs_2_.refs_1_), channel_id=1, source_target_pairs={{0,16},{8,24},{16,0},{24,8},{1,17},{9,25},{17,1},{25,9},{2,18},{10... | collective-permute-start | bytes 3145736 | tf_op jit(solution)/shard_map/ppermute | solution.py:335
  149.2 24.4 %collective-permute-start.12 = (bf16[16,2,128,128]{3,2,1,0:T(8,128)(2,1)}, bf16[16,2,128,128]{3,2,1,0:T(8,128)(2,1)S(1)}, u32[]{:S(2)}, u32[]{:S(2)}) collective-permute-start(bf16[16,2,128,128]{3,2,1,0:T(8,128)(2,1)} %collective-permute-done.6.refs_7_.refs_6_), channel_id=1, source_target_pairs={{0,8},{8,0},{16,24},{24,16},{1,9},{9,1},{17,25},{25,17},{2,10},{10... | collective-permute-start | bytes 3145736 | tf_op jit(solution)/shard_map/ppermute | solution.py:335
  172.0 25.0 %collective-permute-start.13 = (bf16[2,8,2,128,128]{4,3,2,1,0:T(8,128)(2,1)}, bf16[2,8,2,128,128]{4,3,2,1,0:T(8,128)(2,1)S(1)}, u32[]{:S(2)}, u32[]{:S(2)}) collective-permute-start(bf16[2,8,2,128,128]{4,3,2,1,0:T(8,128)(2,1)} %get-tuple-element.61), channel_id=1, source_target_pairs={{0,16},{8,24},{16,0},{24,8},{1,17},{9,25},{17,1},{25,9},{2,18},{10... | collective-permute-start | bytes 3145736 | tf_op jit(solution)/shard_map/ppermute | solution.py:335
  173.6 1.3 copy-start.6
  197.0 11.4 %copy-start.10 = (bf16[2,8,2,128,128]{4,3,2,1,0:T(8,128)(2,1)}, bf16[2,8,2,128,128]{4,3,2,1,0:T(8,128)(2,1)S(1)}, u32[]{:S(2)}) copy-start(bf16[2,8,2,128,128]{4,3,2,1,0:T(8,128)(2,1)S(1)} %collective-permute-done.13.refs_0_) | copy-start | bytes 3145732
  197.1 27.3 %collective-permute-start.16 = (bf16[2,8,2,128,128]{4,3,2,1,0:T(8,128)(2,1)}, bf16[2,8,2,128,128]{4,3,2,1,0:T(8,128)(2,1)S(1)}, u32[]{:S(2)}, u32[]{:S(2)}) collective-permute-start(bf16[2,8,2,128,128]{4,3,2,1,0:T(8,128)(2,1)} %get-tuple-element.55), channel_id=1, source_target_pairs={{0,16},{8,24},{16,0},{24,8},{1,17},{9,25},{17,1},{25,9},{2,18},{10... | collective-permute-start | bytes 3145736 | tf_op jit(solution)/shard_map/ppermute | solution.py:335
  208.5 37.4 %collective-permute-start.15 = (bf16[2,8,2,128,128]{4,3,2,1,0:T(8,128)(2,1)}, bf16[2,8,2,128,128]{4,3,2,1,0:T(8,128)(2,1)S(1)}, u32[]{:S(2)}, u32[]{:S(2)}) collective-permute-start(bf16[2,8,2,128,128]{4,3,2,1,0:T(8,128)(2,1)} %get-tuple-element.65), channel_id=1, source_target_pairs={{0,16},{8,24},{16,0},{24,8},{1,17},{9,25},{17,1},{25,9},{2,18},{10... | collective-permute-start | bytes 3145736 | tf_op jit(solution)/shard_map/ppermute | solution.py:335
  220.9 43.5 %collective-permute-start.14 = (bf16[2,8,2,128,128]{4,3,2,1,0:T(8,128)(2,1)}, bf16[2,8,2,128,128]{4,3,2,1,0:T(8,128)(2,1)S(1)}, u32[]{:S(2)}, u32[]{:S(2)}) collective-permute-start(bf16[2,8,2,128,128]{4,3,2,1,0:T(8,128)(2,1)} %get-tuple-element.68), channel_id=1, source_target_pairs={{0,16},{8,24},{16,0},{24,8},{1,17},{9,25},{17,1},{25,9},{2,18},{10... | collective-permute-start | bytes 3145736 | tf_op jit(solution)/shard_map/ppermute | solution.py:335
  245.9 1.0 copy-start.11
  (4 other events, 3.8 us)
Sparse Core Ops, SparseCore 0:
  10.3 67.4 all-gather.2
  79.4 64.7 all-gather.4
  197.2 69.1 reduce-scatter.1
